TPU v7x, 32 devices: a whole 2x2x4 slice. The times are simulated.
32 devices in a mesh: dp: 16 (over z, x, core), spk: 2 (over y).
Axes of the slice: x: 2, y: 2, z: 4, core: 2. Of those that a mesh axis runs over, the one named last changes fastest.
Arguments:
- spans: bfloat16 [512, 100, 64], P(('dp', 'spk')), may hold values from -6 to 6
- encoded: bfloat16 [25600, 64], P(('dp', 'spk')), may hold values from -6 to 6
- clip_lengths: int32 [16, 2, 3], P('dp'), may hold values from 1 to 12, 16 in all within a row
- clip_pads: int32 [16, 2, 3], P('dp'), may hold values from 0 to 49
- lstm_in: bfloat16 [2, 2, 2, 64, 512], replicated, may hold values from -0.75 to 0.75
- lstm_rec: bfloat16 [2, 2, 2, 128, 512], replicated, may hold values from -0.5 to 0.5
- lstm_bias: float32 [2, 2, 2, 512], replicated, may hold values from -3 to 3
- proj_weight: bfloat16 [2, 2, 256, 64], replicated, may hold values from -0.375 to 0.375
- proj_bias: float32 [2, 2, 64], replicated, may hold values from -3 to 3
- gln_gain: float32 [2, 2, 64], replicated, may hold values from 0.25 to 1.75
- gln_shift: float32 [2, 2, 64], replicated, may hold values from -3 to 3
- mask_weight: bfloat16 [2, 64, 64], P('spk'), may hold values from -0.75 to 0.75
- mask_bias: bfloat16 [2, 64], P('spk'), may hold values from -3 to 3
- dec_weight: bfloat16 [64, 16], replicated, may hold values from -0.75 to 0.75
- wave_grad: bfloat16 [2, 204800], P('spk', 'dp'), may hold values from -6 to 6
Outputs:
- waveforms: float32 [2, 204800], P('spk', 'dp')
- grad_spans: float32 [512, 100, 64], P(('dp', 'spk'))
- grad_lstm_in: float32 [2, 2, 2, 64, 512], replicated
- grad_lstm_rec: float32 [2, 2, 2, 128, 512], replicated
- grad_lstm_bias: float32 [2, 2, 2, 512], replicated
- grad_proj_weight: float32 [2, 2, 256, 64], replicated
- grad_proj_bias: float32 [2, 2, 64], replicated
- grad_gln_gain: float32 [2, 2, 64], replicated
- grad_gln_shift: float32 [2, 2, 64], replicated
- grad_mask_weight: float32 [2, 64, 64], P('spk')
- grad_mask_bias: float32 [2, 64], P('spk')
- grad_dec_weight: float32 [64, 16], replicated
Inputs may be any that keep to these rules, and one draw needn't show every extreme that they name: `clip_lengths`: each device's 3 counts sum to 16, and on every device the longest is exactly 12.
All inputs are finite; a program needn't handle non-finite values.
Results may differ from a plain program's by a relative error of at most 0.013.
Values may be sent and summed in bfloat16 or wider, within the bound.
A program may use at most 192 MiB of HBM per device.

v0:
```python
import functools

import jax
import jax.numpy as jnp
from jax import lax
from jax.experimental import pallas as pl
from jax.experimental.pallas import tpu as pltpu
from jax.sharding import PartitionSpec as P

F32 = jnp.float32
BF16 = jnp.bfloat16
LANES = 128


def dot(a, b):
    return jnp.dot(a, b, preferred_element_type=F32)


def dot_tn(a, b):
    return lax.dot_general(a, b, (((0,), (0,)), ((), ())), preferred_element_type=F32)


def dot_nt(a, b):
    return lax.dot_general(a, b, (((1,), (1,)), ((), ())), preferred_element_type=F32)


def chunks(total, size, body):
    assert total % size == 0

    def step(i, carry):
        body(pl.multiple_of(i * size, size))
        return carry

    lax.fori_loop(0, total // size, step, 0)


def local_kernel(
    sizes,
    lengths_ref,
    pads_ref,
    spans_ref,
    enc_ref,
    w_in_ref,
    w_rec_ref,
    w_bias_ref,
    w_proj_ref,
    proj_bias_ref,
    gain_ref,
    shift_ref,
    mask_ref,
    mask_bias_ref,
    dec_ref,
    dw_ref,
    wave_out,
    spans_out,
    in_out,
    rec_out,
    bias_out,
    proj_out,
    proj_bias_out,
    gain_out,
    shift_out,
    mask_out,
    mask_bias_out,
    dec_out,
    stream,
    valid,
    mx,
    xj,
    dz,
    dmj,
    normed,
    inv_all,
    u_a,
    u_e,
    hc_a,
    hc_e,
    sv_a,
    sv_e,
    gd,
    dh,
    dp,
    wis,
    wrs,
    wiu,
    wrt,
    pws,
    vec,
    enc_t,
    pre,
    masked,
    feats,
    dpre,
):
    R, K, C, H, clips, blocks, kp = sizes
    rows, rows_e = R * K, R * kp
    hop = K // 2
    frames = R * hop
    half = 8
    cr = 10 * R
    speaker = lax.axis_index("spk")

    jio = lax.broadcasted_iota(jnp.int32, (R, LANES), 0)
    lane = lax.broadcasted_iota(jnp.int32, (1, LANES), 1)
    ones_lane = (lane == C).astype(F32)

    lens = [lengths_ref[0, speaker, c] for c in range(clips)]
    pads = [pads_ref[0, speaker, c] for c in range(clips)]
    starts, ends, at = [], [], 0
    for c in range(clips):
        starts.append(at)
        at = at + lens[c]
        ends.append(at)

    def is_start(j):
        hit = j == starts[0]
        for c in range(1, clips):
            hit = jnp.logical_or(hit, j == starts[c])
        return hit

    def is_end(j):
        hit = j == ends[0] - 1
        for c in range(1, clips):
            hit = jnp.logical_or(hit, j == ends[c] - 1)
        return hit

    members, thr, inv_count = [], jnp.full((R, LANES), K, jnp.int32), jnp.zeros((R, LANES), F32)
    for c in range(clips):
        member = jnp.logical_and(jio >= starts[c], jio < ends[c]).astype(F32)
        members.append(member)
        thr = jnp.where(jio == ends[c] - 1, K - pads[c], thr)
        total = (C * (K * lens[c] - pads[c])).astype(F32)
        inv_count = inv_count + member / jnp.full((R, LANES), total, F32)
    not_first = 1.0 - is_start(jio).astype(F32)
    next_not_first = 1.0 - jnp.logical_or(is_start(jio + 1), jio == R - 1).astype(F32)

    def clip_sum(x):
        out = jnp.zeros((R, 1), F32)
        for member in members:
            out = out + member[:, :1] * jnp.sum(member * x, axis=(0, 1), keepdims=True)
        return out

    def fill_valid(r):
        k = lax.broadcasted_iota(jnp.int32, (cr // R, R, LANES), 0) + r // R
        low = lax.broadcasted_iota(jnp.int32, (cr // R, R, LANES), 2) < C
        ok = jnp.logical_and(k < thr[None], low).astype(F32)
        valid[pl.ds(r, cr)] = ok.reshape(cr, LANES)

    chunks(rows, cr, fill_valid)

    pws[...] = jnp.zeros_like(pws)
    wis[...] = jnp.zeros_like(wis)
    wiu[...] = jnp.zeros_like(wiu)
    vec[...] = jnp.zeros_like(vec)
    for b in range(blocks):
        for s in range(2):
            n = 2 * b + s
            pws[b, s, :, 0:C] = w_proj_ref[b, s]
            vec[n, 0:1, 0:C] = proj_bias_ref[b, s : s + 1]
            vec[n, 1:2, 0:C] = gain_ref[b, s : s + 1]
            vec[n, 2:3, 0:C] = shift_ref[b, s : s + 1]

    stream[...] = jnp.zeros_like(stream)
    for j in range(R):
        x = spans_ref[j].astype(F32)
        stream[pl.ds(j, K, stride=R), :] = jnp.concatenate([x, jnp.zeros_like(x)], axis=1)

    def start_stream(r):
        x = stream[pl.ds(r, cr)] * valid[pl.ds(r, cr)]
        stream[pl.ds(r, cr)] = jnp.where(lane == C, 1.0, x)

    chunks(rows, cr, start_stream)

    gate_scale = jnp.where(
        lax.broadcasted_iota(jnp.int32, (1, 4 * H), 1) // H == 2, 1.0, 0.5
    ).astype(F32)

    def lane_part(x, g):
        return x[:, g * H : (g + 1) * H]

    def gate_step(d, sv, b, r, n, p, c, keep_next):
        acts = [jnp.tanh(p[:, g * H : (g + 1) * H] + gd[d, pl.ds(r, n), g * H : (g + 1) * H]) for g in range(4)]
        ti, tf, g, to = acts
        i, f, o = 0.5 * ti + 0.5, 0.5 * tf + 0.5, 0.5 * to + 0.5
        cn = f * c + i * g
        tc = jnp.tanh(cn)
        h = o * tc
        parts = [
            g * (0.25 - 0.25 * ti * ti),
            c * (0.25 - 0.25 * tf * tf),
            i * (1.0 - g * g),
            tc * (0.25 - 0.25 * to * to),
            o * (1.0 - tc * tc),
            f,
        ]
        for m, part in enumerate(parts):
            sv[b, d, pl.ds(r, n), m * H : (m + 1) * H] = part.astype(BF16)
        if keep_next is None:
            return h.astype(BF16), h.astype(BF16), cn
        return h.astype(BF16), (h * keep_next).astype(BF16), cn * keep_next

    def run_forward(b, sec, u, hc, sv, n, steps, unroll):
        total = n * steps
        for d in range(2):
            w = w_in_ref[b, sec, d].astype(F32) * gate_scale
            wis[0:C, d * 4 * H : (d + 1) * 4 * H] = w.astype(BF16)
            wrs[d] = (w_rec_ref[b, sec, d].astype(F32) * gate_scale).astype(BF16)
        size = total // 4

        def drive(r):
            for d in range(2):
                bias = w_bias_ref[b, sec, d : d + 1] * gate_scale
                gd[d, pl.ds(r, size)] = (
                    dot(u[b, pl.ds(r, size)], wis[:, d * 4 * H : (d + 1) * 4 * H]) + bias
                )

        chunks(total, size, drive)

        def step(t, carry):
            hf, hb, cf, cb = carry
            back = steps - 1 - t
            rf = pl.multiple_of(t * n, n)
            rb = pl.multiple_of(back * n, n)
            kf = kb = None
            if sec == 1:
                kf = 1.0 - is_start(t + 1).astype(F32)
                kb = 1.0 - is_end(back - 1).astype(F32)
            pf = dot(hf, wrs[0])
            pb = dot(hb, wrs[1])
            out_f, hf, cf = gate_step(0, sv, b, rf, n, pf, cf, kf)
            out_b, hb, cb = gate_step(1, sv, b, rb, n, pb, cb, kb)
            hc[b, pl.ds(rf, n), 0:H] = out_f
            hc[b, pl.ds(rb, n), H : 2 * H] = out_b
            return hf, hb, cf, cb

        zh, zc = jnp.zeros((n, H), BF16), jnp.zeros((n, H), F32)
        lax.fori_loop(0, steps, step, (zh, zh, zc, zc), unroll=unroll)

    def norm_forward(b, sec):
        n = 2 * b + sec
        gain, shift = vec[n, 1:2], vec[n, 2:3]

        def fold(body):
            def step(i, acc):
                return acc + jnp.sum(body(pl.multiple_of(i * cr, cr)).reshape(cr // R, R, LANES), axis=0)

            return lax.fori_loop(0, rows // cr, step, jnp.zeros((R, LANES), F32))

        mean = clip_sum(fold(lambda r: valid[pl.ds(r, cr)] * mx[pl.ds(r, cr)])) * inv_count

        def spread(r):
            x = mx[pl.ds(r, cr)].reshape(cr // R, R, LANES) - mean[None]
            return valid[pl.ds(r, cr)] * (x * x).reshape(cr, LANES)

        inv = lax.rsqrt(clip_sum(fold(spread)) * inv_count + 1e-08)
        inv_all[n] = inv

        def apply(r):
            x = (mx[pl.ds(r, cr)].reshape(cr // R, R, LANES) - mean[None]) * inv[None]
            x = x.reshape(cr, LANES)
            normed[n, pl.ds(r, cr)] = x
            stream[pl.ds(r, cr)] += valid[pl.ds(r, cr)] * (x * gain + shift)

        chunks(rows, cr, apply)

    def forward_block(b, carry):
        def u_intra(r):
            u_a[b, pl.ds(r, cr)] = stream[pl.ds(r, cr)].astype(BF16)

        chunks(rows, cr, u_intra)
        run_forward(b, 0, u_a, hc_a, sv_a, R, K, 4)

        def mix_intra(r):
            mx[pl.ds(r, rows // 4)] = dot(hc_a[b, pl.ds(r, rows // 4)], pws[b, 0]) + vec[2 * b, 0:1]

        chunks(rows, rows // 4, mix_intra)
        norm_forward(b, 0)

        for j in range(R):
            u_e[b, pl.ds(j * kp, kp)] = stream[pl.ds(j, kp, stride=R), :].astype(BF16)
        run_forward(b, 1, u_e, hc_e, sv_e, kp, R, 2)

        def mix_inter(r):
            xj[pl.ds(r, rows_e // 4)] = (
                dot(hc_e[b, pl.ds(r, rows_e // 4)], pws[b, 1]) + vec[2 * b + 1, 0:1]
            )

        chunks(rows_e, rows_e // 4, mix_inter)
        for j in range(R):
            mx[pl.ds(j, kp, stride=R), :] = xj[pl.ds(j * kp, kp)]
        norm_forward(b, 1)
        return carry

    lax.fori_loop(0, blocks, forward_block, 0)

    for j in range(R):
        e = enc_ref[j * hop : (j + 1) * hop].astype(F32)
        enc_t[pl.ds(j, hop, stride=R), :] = jnp.concatenate([e, e], axis=1)
        xj[pl.ds(j, hop, stride=R), :] = dw_ref[j * hop : (j + 1) * hop]
    seg_a, seg_b = 2, 3

    def head_pre(r):
        x = stream[pl.ds(r, cr)]
        f = x * (0.5 * jnp.tanh(0.5 * x) + 0.5)
        f = jnp.where(lane == C, 1.0, f).astype(BF16)
        feats[pl.ds(r, cr)] = f
        pre[pl.ds(r, cr)] = dot(f[:, 0:C], mask_ref[...]) + mask_bias_ref[...]

    chunks(rows, cr, head_pre)

    hr = frames // 5
    del seg_a, seg_b

    def tile(v):
        return jnp.broadcast_to(v[None], (hr // R, R, LANES)).reshape(hr, LANES)

    for q in range(5):
        r = q * hr
        fr = pre[r : r + hr] + tile(not_first) * pre[frames + r - 1 : frames + r - 1 + hr]
        e = enc_t[r : r + hr]
        sp = jnp.maximum(fr, 0.0) + jnp.log1p(jnp.exp(-jnp.abs(fr)))
        masked[r : r + hr] = (sp * e).astype(BF16)
        pre[r : r + hr] = e * (0.5 * jnp.tanh(0.5 * fr) + 0.5)
    for q in range(5):
        r = q * hr
        gd[0, r : r + hr, 0 : 2 * LANES] = dot(masked[r : r + hr], dec_ref[...])
    gd[1, 0:R, 0:LANES] = (
        gd[0, 0:R, 0:LANES] + not_first * gd[0, frames - R - 1 : frames - 1, LANES : 2 * LANES]
    )
    gd[1, R:frames, 0:LANES] = gd[0, R:frames, 0:LANES] + gd[0, 0 : frames - R, LANES : 2 * LANES]
    xj[frames : 2 * frames] = gd[1, 0:frames, 0:LANES]
    for j in range(R):
        wave_out[j * hop : (j + 1) * hop] = xj[pl.ds(frames + j, hop, stride=R), :][:, 0 : 2 * half]

    gd[0, 0:frames, 0:LANES] = xj[0:frames]
    gd[0, 0 : frames - R, LANES : 2 * LANES] = xj[R:frames]
    gd[0, frames - R : frames, LANES : 2 * LANES] = next_not_first * xj[1 : R + 1]
    dp[0, 0:frames, 0 : 2 * LANES] = gd[0, 0:frames, 0 : 2 * LANES].astype(BF16)
    dec_out[...] = dot_tn(masked[...], dp[0, 0:frames, 0 : 2 * LANES])
    xj[frames : frames + 8] = jnp.zeros((8, LANES), F32)
    for q in range(5):
        r = q * hr
        dfr = dot_nt(dp[0, r : r + hr, 0 : 2 * LANES], dec_ref[...]) * pre[r : r + hr]
        xj[r : r + hr] = dfr
        dpre[r : r + hr] = dfr.astype(BF16)
    for q in range(5):
        r = q * hr
        dpre[frames + r : frames + r + hr] = (tile(next_not_first) * xj[r + 1 : r + 1 + hr]).astype(BF16)
    gm = dot_tn(feats[...], dpre[...])
    mask_out[...] = gm[0:C]
    mask_bias_out[...] = gm[C : C + 1]
    dz[...] = jnp.zeros_like(dz)

    def head_dz(r):
        x = stream[pl.ds(r, cr)]
        sg = 0.5 * jnp.tanh(0.5 * x) + 0.5
        df = dot_nt(dpre[pl.ds(r, cr)], mask_ref[...])
        df = jnp.concatenate([df, jnp.zeros_like(df)], axis=1)
        dz[pl.ds(r, cr)] = df * sg * (1.0 + x * (1.0 - sg))

    chunks(rows, cr, head_dz)

    def norm_backward(b, sec):
        n = 2 * b + sec
        gain = vec[n, 1:2]

        def sums(i, acc):
            r = pl.multiple_of(i * cr, cr)
            v = valid[pl.ds(r, cr)] * dz[pl.ds(r, cr)]
            w = v * normed[n, pl.ds(r, cr)]
            return (
                acc[0] + jnp.sum(v.reshape(cr // R, R, LANES), axis=0),
                acc[1] + jnp.sum(w.reshape(cr // R, R, LANES), axis=0),
            )

        zero = jnp.zeros((R, LANES), F32)
        s1, s2 = lax.fori_loop(0, rows // cr, sums, (zero, zero))
        shift_out[b, sec : sec + 1] = jnp.sum(s1, axis=0, keepdims=True)[:, 0:C]
        gain_out[b, sec : sec + 1] = jnp.sum(s2, axis=0, keepdims=True)[:, 0:C]
        m1 = clip_sum(s1 * gain) * inv_count
        m2 = clip_sum(s2 * gain) * inv_count
        inv = inv_all[n]

        def apply(i, acc):
            r = pl.multiple_of(i * cr, cr)
            d = (dz[pl.ds(r, cr)] * gain).reshape(cr // R, R, LANES)
            x = normed[n, pl.ds(r, cr)].reshape(cr // R, R, LANES)
            y = (d - m1[None] - x * m2[None]) * inv[None]
            y = (y.reshape(cr, LANES) * valid[pl.ds(r, cr)]).astype(BF16)
            if sec == 0:
                dmj[pl.ds(r, cr)] = y
            y = y.astype(F32)
            if sec == 1:
                mx[pl.ds(r, cr)] = y
            return acc + jnp.sum(y.reshape(cr // R, R, LANES), axis=0)

        acc = lax.fori_loop(0, rows // cr, apply, zero)
        proj_bias_out[b, sec : sec + 1] = jnp.sum(acc, axis=0, keepdims=True)[:, 0:C]

    def back_step(d, sv, b, r, n, dhn, dcn, keep):
        a = [sv[b, d, pl.ds(r, n), m * H : (m + 1) * H].astype(F32) for m in range(6)]
        g = dh[pl.ds(r, n), d * H : (d + 1) * H] + dhn
        dc = dcn + g * a[4]
        for m in range(4):
            dp[d, pl.ds(r, n), m * H : (m + 1) * H] = ((g if m == 3 else dc) * a[m]).astype(BF16)
        dhn = dot(dp[d, pl.ds(r, n)], wrt[d])
        dcn = dc * a[5]
        if keep is not None:
            dhn, dcn = dhn * keep, dcn * keep
        return dhn, dcn

    def run_backward(b, sec, u, hc, sv, n, steps, unroll):
        total = n * steps
        size = total // 4
        proj_out[b, sec] = dot_tn(dmj[0:total], hc[b]).T[:, 0:C]

        def joined(r):
            dh[pl.ds(r, size)] = dot_nt(dmj[pl.ds(r, size)], pws[b, sec])

        chunks(total, size, joined)
        for d in range(2):
            wrt[d] = w_rec_ref[b, sec, d].T
            wiu[0:C, d * 4 * H : (d + 1) * 4 * H] = w_in_ref[b, sec, d]

        def step(t, carry):
            hf, hb, cf, cb = carry
            back = steps - 1 - t
            rf = pl.multiple_of(back * n, n)
            rb = pl.multiple_of(t * n, n)
            kf = kb = None
            if sec == 1:
                kf = 1.0 - is_start(back).astype(F32)
                kb = 1.0 - is_end(t).astype(F32)
            hf, cf = back_step(0, sv, b, rf, n, hf, cf, kf)
            hb, cb = back_step(1, sv, b, rb, n, hb, cb, kb)
            return hf, hb, cf, cb

        z = jnp.zeros((n, H), F32)
        lax.fori_loop(0, steps, step, (z, z, z, z), unroll=unroll)
        if sec == 1:
            for j in range(1, steps):
                kf = (1.0 - is_start(j).astype(F32)).astype(BF16)
                at = slice((j - 1) * n, j * n)
                hc[b, at, 0:H] = hc[b, at, 0:H] * kf
                kb = (1.0 - is_end(j - 1).astype(F32)).astype(BF16)
                at = slice(j * n, (j + 1) * n)
                hc[b, at, H : 2 * H] = hc[b, at, H : 2 * H] * kb
        for d in range(2):
            g = dot_tn(u[b], dp[d, 0:total])
            in_out[b, sec, d] = g[0:C]
            bias_out[b, sec, d : d + 1] = g[C : C + 1]
        rec_out[b, sec, 0] = dot_tn(hc[b, 0 : total - n, 0:H], dp[0, n:total])
        rec_out[b, sec, 1] = dot_tn(hc[b, n:total, H : 2 * H], dp[1, 0 : total - n])

    def stream_grad(r, size):
        return dot_nt(dp[0, pl.ds(r, size)], wiu[:, 0 : 4 * H]) + dot_nt(
            dp[1, pl.ds(r, size)], wiu[:, 4 * H : 8 * H]
        )

    def backward_block(i, carry):
        b = blocks - 1 - i
        norm_backward(b, 1)
        mx[rows:rows_e] = jnp.zeros((rows_e - rows, LANES), F32)
        for j in range(R):
            dmj[pl.ds(j * kp, kp)] = mx[pl.ds(j, kp, stride=R), :].astype(BF16)
        run_backward(b, 1, u_e, hc_e, sv_e, kp, R, 2)

        def grad_inter(r):
            xj[pl.ds(r, rows_e // 4)] = stream_grad(r, rows_e // 4)

        chunks(rows_e, rows_e // 4, grad_inter)
        for j in range(R):
            dz[pl.ds(j, kp, stride=R), :] += xj[pl.ds(j * kp, kp)]

        norm_backward(b, 0)
        run_backward(b, 0, u_a, hc_a, sv_a, R, K, 4)

        def grad_intra(r):
            dz[pl.ds(r, rows // 4)] += stream_grad(r, rows // 4)

        chunks(rows, rows // 4, grad_intra)
        return carry

    lax.fori_loop(0, blocks, backward_block, 0)

    def finish(r):
        dz[pl.ds(r, cr)] = dz[pl.ds(r, cr)] * valid[pl.ds(r, cr)]

    chunks(rows, cr, finish)
    for j in range(R):
        spans_out[j] = dz[pl.ds(j, K, stride=R), :][:, 0:C]


def shards(
    spans,
    encoded,
    clip_lengths,
    clip_pads,
    lstm_in,
    lstm_rec,
    lstm_bias,
    proj_weight,
    proj_bias,
    gln_gain,
    gln_shift,
    mask_weight,
    mask_bias,
    dec_weight,
    wave_grad,
):
    speaker = lax.axis_index("spk")
    R, K, C = spans.shape
    H = lstm_rec.shape[3]
    blocks = lstm_in.shape[0]
    clips = clip_lengths.shape[2]
    frames = encoded.shape[0]
    half = dec_weight.shape[1] // 2
    samples = frames * half
    kp = -(-K // 16) * 16
    rows, rows_e = R * K, R * kp

    mine = lax.dynamic_slice_in_dim(wave_grad[0], speaker * samples, samples, 0)
    theirs = lax.dynamic_slice_in_dim(wave_grad[0], (1 - speaker) * samples, samples, 0)
    sent = jnp.concatenate([theirs, mask_weight.reshape(-1), mask_bias.reshape(-1)])
    got = lax.ppermute(sent, "spk", [(0, 1), (1, 0)])
    other_mask = got[samples : samples + C * C].reshape(C, C)
    other_bias = got[samples + C * C :].reshape(1, C)
    dw = jnp.concatenate([mine.reshape(frames, half), got[:samples].reshape(frames, half)], axis=1)
    dw = jnp.pad(dw.astype(F32), ((0, 0), (0, LANES - 2 * half)))
    masks = jnp.concatenate([mask_weight[0], other_mask], axis=1)
    mask_biases = jnp.concatenate([mask_bias, other_bias], axis=1).astype(F32)
    zero = jnp.zeros((C, half), BF16)
    pad = jnp.zeros((C, LANES - 2 * half), BF16)
    lead, tail = dec_weight[:, :half], dec_weight[:, half:]
    dec = jnp.concatenate(
        [
            jnp.concatenate([lead, zero, pad, tail, zero, pad], axis=1),
            jnp.concatenate([zero, lead, pad, zero, tail, pad], axis=1),
        ],
        axis=0,
    )

    sizes = (R, K, C, H, clips, blocks, kp)
    smem = pl.BlockSpec(memory_space=pltpu.SMEM)
    vmem = pl.BlockSpec(memory_space=pltpu.VMEM)
    shape = jax.ShapeDtypeStruct
    outs = pl.pallas_call(
        functools.partial(local_kernel, sizes),
        out_shape=(
            shape((frames, 2 * half), F32),
            shape((R, K, C), F32),
            shape((blocks, 2, 2, C, 4 * H), F32),
            shape((blocks, 2, 2, H, 4 * H), F32),
            shape((blocks, 2, 2, 4 * H), F32),
            shape((blocks, 2, 2 * H, C), F32),
            shape((blocks, 2, C), F32),
            shape((blocks, 2, C), F32),
            shape((blocks, 2, C), F32),
            shape((C, 2 * C), F32),
            shape((1, 2 * C), F32),
            shape((2 * C, 2 * LANES), F32),
        ),
        in_specs=[smem, smem] + [vmem] * 13,
        out_specs=tuple([vmem] * 12),
        scratch_shapes=[
            pltpu.VMEM((rows_e, LANES), F32),
            pltpu.VMEM((rows, LANES), F32),
            pltpu.VMEM((rows_e, LANES), F32),
            pltpu.VMEM((rows_e, LANES), F32),
            pltpu.VMEM((rows_e, LANES), F32),
            pltpu.VMEM((rows_e, LANES), BF16),
            pltpu.VMEM((2 * blocks, rows, LANES), F32),
            pltpu.VMEM((2 * blocks, R, LANES), F32),
            pltpu.VMEM((blocks, rows, LANES), BF16),
            pltpu.VMEM((blocks, rows_e, LANES), BF16),
            pltpu.VMEM((blocks, rows, 2 * H), BF16),
            pltpu.VMEM((blocks, rows_e, 2 * H), BF16),
            pltpu.VMEM((blocks, 2, rows, 6 * H), BF16),
            pltpu.VMEM((blocks, 2, rows_e, 6 * H), BF16),
            pltpu.VMEM((2, rows_e, 4 * H), F32),
            pltpu.VMEM((rows_e, 2 * H), F32),
            pltpu.VMEM((2, rows_e, 4 * H), BF16),
            pltpu.VMEM((LANES, 8 * H), BF16),
            pltpu.VMEM((2, H, 4 * H), BF16),
            pltpu.VMEM((LANES, 8 * H), BF16),
            pltpu.VMEM((2, 4 * H, H), BF16),
            pltpu.VMEM((blocks, 2, 2 * H, LANES), BF16),
            pltpu.VMEM((2 * blocks, 8, LANES), F32),
            pltpu.VMEM((frames, LANES), F32),
            pltpu.VMEM((rows, LANES), F32),
            pltpu.VMEM((frames, LANES), BF16),
            pltpu.VMEM((rows, LANES), BF16),
            pltpu.VMEM((rows, LANES), BF16),
        ],
        compiler_params=pltpu.CompilerParams(vmem_limit_bytes=62 * 1024 * 1024),
        name="dual_path",
    )(
        clip_lengths,
        clip_pads,
        spans,
        encoded,
        lstm_in,
        lstm_rec,
        lstm_bias,
        proj_weight,
        proj_bias,
        gln_gain,
        gln_shift,
        masks,
        mask_biases,
        dec,
        dw,
    )
    wave, grad_spans = outs[0], outs[1]
    own_wave = wave[:, :half].reshape(-1)
    far_wave = lax.ppermute(wave[:, half:].reshape(-1), "spk", [(0, 1), (1, 0)])
    first = speaker == 0
    waveforms = jnp.where(
        first,
        jnp.concatenate([own_wave, far_wave]),
        jnp.concatenate([far_wave, own_wave]),
    )[None]

    def by_speaker(x):
        a, b = x[:, :C], x[:, C:]
        return jnp.where(first, jnp.stack([a, b]), jnp.stack([b, a]))

    gd = outs[11]
    grad_dec = jnp.concatenate(
        [
            gd[:C, :half] + gd[C:, half : 2 * half],
            gd[:C, LANES : LANES + half] + gd[C:, LANES + half : LANES + 2 * half],
        ],
        axis=1,
    )
    summed = lax.psum(
        outs[2:9] + (by_speaker(outs[9]), by_speaker(outs[10])[:, 0], grad_dec), ("dp", "spk")
    )
    return (
        (waveforms, grad_spans)
        + summed[:7]
        + (
            lax.dynamic_slice_in_dim(summed[7], speaker, 1, 0),
            lax.dynamic_slice_in_dim(summed[8], speaker, 1, 0),
            summed[9],
        )
    )


def solution(mesh):
    return jax.shard_map(
        shards,
        mesh=mesh,
        in_specs=(
            P(("dp", "spk"), None, None),
            P(("dp", "spk"), None),
            P("dp", None, None),
            P("dp", None, None),
            P(),
            P(),
            P(),
            P(),
            P(),
            P(),
            P(),
            P("spk", None, None),
            P("spk", None),
            P(),
            P("spk", "dp"),
        ),
        out_specs=(
            P("spk", "dp"),
            P(("dp", "spk"), None, None),
            P(),
            P(),
            P(),
            P(),
            P(),
            P(),
            P(),
            P("spk", None, None),
            P("spk", None),
            P(),
        ),
        check_vma=False,
    )
```

profile of v0, /device:TPU:0, one launch (start us, length us, event | category | flops | bytes accessed | tf_op | source)
XLA Modules:
  0.0 296.2 jit_solution(15515325852043370937)
XLA Ops:
  7.3 0.8 reshape.177
  8.1 0.9 dynamic-slice_reduce_fusion
  9.0 0.7 pad_maximum_fusion.1
  9.6 3.0 %collective-permute-start = (bf16[10560]{0:T(1024)(128)(2,1)S(1)}, bf16[10560]{0:T(1024)(128)(2,1)S(1)}, u32[]{:S(2)}, u32[]{:S(2)}) collective-permute-start(bf16[10560]{0:T(1024)(128)(2,1)S(1)} %pad_maximum_fusion.1), channel_id=1, source_target_pairs={{0,1},{1,0},{2,3},{3,2},{4,5},{5,4},{6,7},{7,6},{8,9},{9,8},{10,11... | collective-permute-start | bytes 63368 | tf_op jit(solution)/shard_map/ppermute | solution.py:525
  12.6 0.7 fusion.5
  13.3 0.1 copy.64
  13.4 0.1 copy.65
  13.5 0.1 concatenate.69
  13.6 0.1 concatenate.68
  13.7 0.6 pad_maximum_fusion.dec_ref
  14.4 1.9 copy.57.spans_ref
  16.3 1.7 copy.58.enc_ref
  18.0 1.7 copy.59.w_proj_ref
  19.8 0.3 reshape.180
  20.2 0.6 maximum_convert_fusion.mask_bias_ref
  20.7 0.3 reshape.181
  21.0 0.7 pad_maximum_fusion.2.mask_ref
  21.7 0.9 fusion.3.dw_ref
  22.6 116.2 %dual_path.1 = (f32[800,16]{1,0:T(8,128)}, f32[16,100,64]{2,1,0:T(8,128)}, f32[2,2,2,64,512]{4,3,2,1,0:T(8,128)}, f32[2,2,2,128,512]{4,3,2,1,0:T(8,128)}, f32[2,...) custom-call(s32[1,2,3]{2,1,0:T(2,128)} %lengths_ref.1, ...), custom_call_target="tpu_custom_call" | custom-call | tf_op jit(solution)/shard_map/dual_path/pallas_call | solution.py:547
  138.9 1.3 fusion.4
  140.2 0.2 reshape.182
  141.0 0.3 copy-done.5
  141.3 43.4 %all-reduce.1 = (f32[2,2,2,512]{3,2,1,0:T(2,128)}, f32[2,2,64]{2,1,0:T(2,128)}, f32[2,2,64]{2,1,0:T(2,128)}, f32[2,2,64]{2,1,0:T(2,128)}, f32[2,64,64]{2,1,0:T(8...) all-reduce(f32[2,2,2,512]{3,2,1,0:T(2,128)S(1)} %copy-done.5, ...), channel_id=1, replica_groups=mesh['dp'=16,'spk'=2] {'dp','spk'}, use_global_device_ids=true, to_apply=%region_2.3 | all-reduce | flops 14208 | bytes 113664 | tf_op jit(solution)/shard_map/psum | solution.py:636
  184.7 0.6 constant_dynamic-slice_fusion.1
  185.3 0.5 constant_dynamic-slice_fusion
  185.8 0.2 concatenate.72
  186.1 1.1 copy.62
  187.2 0.7 broadcast_select_fusion
  187.9 95.8 %all-reduce.5.cloned.1.call-done = (f32[2,2,2,64,512]{4,3,2,1,0:T(8,128)}, f32[2,2,2,128,512]{4,3,2,1,0:T(8,128)}, f32[2,2,256,64]{3,2,1,0:T(8,128)}) async-done(((f32[2,2,2,64,512]{4,3,2,1,0:T(8,128)}, f32[2,2,2,128,512]{4,3,2,1,0:T(8,128)}, f32[2,2,256,64]{3,2,1,0:T(8,128)}), (f32[2,2,2,64,512]{4,3,2,1,0:T(8,128)}, f32[2,2,2,128,512]{4,3,2,1,0:T(8,128)}, ...) | async-done | bytes 3407888 | tf_op jit(solution)/shard_map/psum | solution.py:636
  283.7 2.1 copy.63
  285.7 2.3 copy.69
  288.0 1.3 copy.70
  (41 shorter events, 0.7 us)
Async XLA Ops:
  7.2 13.8 %copy-start.4 = (bf16[1,64,64]{2,1,0:T(8,128)(2,1)S(1)}, bf16[1,64,64]{2,1,0:T(8,128)(2,1)}, u32[]{:S(2)}) copy-start(bf16[1,64,64]{2,1,0:T(8,128)(2,1)} %param.26) | copy-start | bytes 24580
  7.2 13.0 %copy-start.10 = (bf16[1,64]{1,0:T(2,128)(2,1)S(1)}, bf16[1,64]{1,0:T(2,128)(2,1)}, u32[]{:S(2)}) copy-start(bf16[1,64]{1,0:T(2,128)(2,1)} %param.27) | copy-start | bytes 388
  7.2 276.5 %all-reduce.5.cloned.1.call-start = ((), (), s32[]{:S(2)}) async-start(), calls=%async_computation | async-start | bytes 7340032 | tf_op jit(solution)/shard_map/psum | solution.py:636
  9.6 10.4 %collective-permute-start = (bf16[10560]{0:T(1024)(128)(2,1)S(1)}, bf16[10560]{0:T(1024)(128)(2,1)S(1)}, u32[]{:S(2)}, u32[]{:S(2)}) collective-permute-start(bf16[10560]{0:T(1024)(128)(2,1)S(1)} %pad_maximum_fusion.1), channel_id=1, source_target_pairs={{0,1},{1,0},{2,3},{3,2},{4,5},{5,4},{6,7},{7,6},{8,9},{9,8},{10,11... | collective-permute-start | bytes 63368 | tf_op jit(solution)/shard_map/ppermute | solution.py:525
  138.8 1.7 copy-start.3
  138.8 1.8 copy-start.9
  138.9 1.8 copy-start.2
  140.4 46.8 %collective-permute-start.1 = (f32[6400]{0:T(1024)S(1)}, f32[6400]{0:T(1024)S(1)}, u32[]{:S(2)}, u32[]{:S(2)}) collective-permute-start(f32[6400]{0:T(1024)S(1)} %reshape.182), channel_id=1, source_target_pairs={{0,1},{1,0},{2,3},{3,2},{4,5},{5,4},{6,7},{7,6},{8,9},{9,8},{10,11... | collective-permute-start | bytes 76808 | tf_op jit(solution)/shard_map/ppermute | solution.py:616
  140.6 0.7 copy-start.5
  140.6 0.7 copy-start.6
  140.6 0.7 copy-start.7
  140.6 0.7 copy-start.8
  140.9 45.2 %copy-start.1 = (f32[16,100,64]{2,1,0:T(8,128)S(1)}, f32[16,100,64]{2,1,0:T(8,128)}, u32[]{:S(2)}) copy-start(f32[16,100,64]{2,1,0:T(8,128)} %get-tuple-element.73) | copy-start | bytes 1228804
  283.7 4.3 %copy-start = (f32[2,2,2,128,512]{4,3,2,1,0:T(8,128)S(1)}, f32[2,2,2,128,512]{4,3,2,1,0:T(8,128)}, u32[]{:S(2)}) copy-start(f32[2,2,2,128,512]{4,3,2,1,0:T(8,128)} %get-tuple-element.109) | copy-start | bytes 6291460
Sparse Core Ops, SparseCore 0:
  141.1 142.5 all-reduce.4
where the time goes:
time: 297 us; the launch traced here: 296 us
  Pallas kernels  116 us (39%)
  waiting for transfers between devices  95.8 us (32%)
  blocking collectives  43.4 us (15%)
  local copies, waits for them, and re-layouts  19.2 us (6%)
  between operations  14.3 us (5%)
  other arithmetic  4.22 us (1%)
  starting transfers between devices  3.08 us (1%)
    pallas_call x1, Pallas kernels, shards(): pl.pallas_call(functools.partial(local_kernel, sizes), out_shape=(shape((...  116 us
    psum x1, waiting for transfers between devices, shards(): lax.psum(outs[2:9] + (by_speaker(outs[9]), by_speaker(outs[10])[:, 0], gr...  95.8 us
    psum x1, blocking collectives, shards(): lax.psum(outs[2:9] + (by_speaker(outs[9]), by_speaker(outs[10])[:, 0], gr...  43.4 us
    unnamed x31, local copies, waits for them, and re-layouts  12.7 us
  transfers between devices with their start and end apart: 3, of which 1 were waited for; matrix products, arithmetic and copies ran while one was open for 4% of the time, Pallas kernels for 0%

commit v1 on v0

--- a/solution.py
+++ b/solution.py
@@ -10,6 +10,7 @@
 F32 = jnp.float32
 BF16 = jnp.bfloat16
 LANES = 128
+MESH = pl.DeviceIdType.MESH
 
 
 def dot(a, b):
@@ -47,10 +48,10 @@
     proj_bias_ref,
     gain_ref,
     shift_ref,
-    mask_ref,
-    mask_bias_ref,
-    dec_ref,
-    dw_ref,
+    mask_in_ref,
+    mask_bias_in_ref,
+    dec_in_ref,
+    wave_grad_ref,
     wave_out,
     spans_out,
     in_out,
@@ -91,14 +92,45 @@
     masked,
     feats,
     dpre,
+    mask_ref,
+    dec_ref,
+    send,
+    own,
+    got,
+    wave_got,
+    sems,
 ):
     R, K, C, H, clips, blocks, kp = sizes
     rows, rows_e = R * K, R * kp
     hop = K // 2
     frames = R * hop
-    half = 8
+    half = dec_in_ref.shape[0] // 2
+    wr = frames * half // LANES
+    group = LANES // half
     cr = 10 * R
     speaker = lax.axis_index("spk")
+    partner = {"spk": 1 - speaker}
+
+    barrier = pltpu.get_barrier_semaphore()
+    pl.semaphore_signal(barrier, inc=1, device_id=partner, device_id_type=MESH)
+
+    mask_row = -(-wr // 8) * 8
+    for i in range(wr):
+        at = pl.multiple_of(speaker * (wr * LANES) + i * LANES, LANES)
+        own[i : i + 1] = wave_grad_ref[0:1, pl.ds(at, LANES)].astype(F32)
+        at = pl.multiple_of((1 - speaker) * (wr * LANES) + i * LANES, LANES)
+        send[i : i + 1] = wave_grad_ref[0:1, pl.ds(at, LANES)].astype(F32)
+    mask_f = mask_in_ref[0].astype(F32)
+    send[wr:mask_row] = jnp.zeros((mask_row - wr, LANES), F32)
+    send[mask_row : mask_row + C] = jnp.concatenate([mask_f, mask_f], axis=1)
+    bias_f = mask_bias_in_ref[0:1].astype(F32)
+    bias_f = jnp.concatenate([bias_f, bias_f], axis=1)
+    send[mask_row + C : mask_row + C + 8] = jnp.broadcast_to(bias_f, (8, LANES))
+    pl.semaphore_wait(barrier, 1)
+    swap = pltpu.make_async_remote_copy(
+        src_ref=send, dst_ref=got, send_sem=sems.at[0], recv_sem=sems.at[1], device_id=partner, device_id_type=MESH
+    )
+    swap.start()
 
     jio = lax.broadcasted_iota(jnp.int32, (R, LANES), 0)
     lane = lax.broadcasted_iota(jnp.int32, (1, LANES), 1)
@@ -155,7 +187,7 @@
     for b in range(blocks):
         for s in range(2):
             n = 2 * b + s
-            pws[b, s, :, 0:C] = w_proj_ref[b, s]
+            pws[b, s, 0:C] = w_proj_ref[b, s]
             vec[n, 0:1, 0:C] = proj_bias_ref[b, s : s + 1]
             vec[n, 1:2, 0:C] = gain_ref[b, s : s + 1]
             vec[n, 2:3, 0:C] = shift_ref[b, s : s + 1]
@@ -163,7 +195,8 @@
     stream[...] = jnp.zeros_like(stream)
     for j in range(R):
         x = spans_ref[j].astype(F32)
-        stream[pl.ds(j, K, stride=R), :] = jnp.concatenate([x, jnp.zeros_like(x)], axis=1)
+        x = jnp.concatenate([x, jnp.zeros_like(x)], axis=0).T
+        stream[pl.ds(j, K, stride=R), :] = x
 
     def start_stream(r):
         x = stream[pl.ds(r, cr)] * valid[pl.ds(r, cr)]
@@ -271,7 +304,7 @@
         run_forward(b, 0, u_a, hc_a, sv_a, R, K, 4)
 
         def mix_intra(r):
-            mx[pl.ds(r, rows // 4)] = dot(hc_a[b, pl.ds(r, rows // 4)], pws[b, 0]) + vec[2 * b, 0:1]
+            mx[pl.ds(r, rows // 4)] = dot_nt(hc_a[b, pl.ds(r, rows // 4)], pws[b, 0]) + vec[2 * b, 0:1]
 
         chunks(rows, rows // 4, mix_intra)
         norm_forward(b, 0)
@@ -282,7 +315,7 @@
 
         def mix_inter(r):
             xj[pl.ds(r, rows_e // 4)] = (
-                dot(hc_e[b, pl.ds(r, rows_e // 4)], pws[b, 1]) + vec[2 * b + 1, 0:1]
+                dot_nt(hc_e[b, pl.ds(r, rows_e // 4)], pws[b, 1]) + vec[2 * b + 1, 0:1]
             )
 
         chunks(rows_e, rows_e // 4, mix_inter)
@@ -293,23 +326,45 @@
 
     lax.fori_loop(0, blocks, forward_block, 0)
 
+    e = enc_ref[...].astype(F32)
+    xj[0:frames] = jnp.concatenate([e, e], axis=0).T
     for j in range(R):
-        e = enc_ref[j * hop : (j + 1) * hop].astype(F32)
-        enc_t[pl.ds(j, hop, stride=R), :] = jnp.concatenate([e, e], axis=1)
-        xj[pl.ds(j, hop, stride=R), :] = dw_ref[j * hop : (j + 1) * hop]
-    seg_a, seg_b = 2, 3
+        enc_t[pl.ds(j, hop, stride=R), :] = xj[j * hop : (j + 1) * hop]
+
+    first_half = lane < half
+    second_half = jnp.logical_and(lane >= half, lane < 2 * half)
+    d = dec_in_ref[...].astype(F32)
+    d = jnp.concatenate([d, jnp.zeros((LANES - 2 * half, C), F32)], axis=0).T
+    dec_ref[0:C, 0:LANES] = jnp.where(first_half, d, 0.0).astype(BF16)
+    dec_ref[C : 2 * C, 0:LANES] = jnp.where(second_half, pltpu.roll(d, half, 1), 0.0).astype(BF16)
+    dec_ref[0:C, LANES : 2 * LANES] = jnp.where(first_half, pltpu.roll(d, LANES - half, 1), 0.0).astype(BF16)
+    dec_ref[C : 2 * C, LANES : 2 * LANES] = jnp.where(second_half, d, 0.0).astype(BF16)
+
+    swap.wait()
+    mask_ref[...] = jnp.concatenate([mask_f, got[mask_row : mask_row + C, 0:C]], axis=1).astype(BF16)
+    mask_bias = jnp.concatenate(
+        [mask_bias_in_ref[0:1].astype(F32), got[mask_row + C : mask_row + C + 1, 0:C]], axis=1
+    )
+    for q in range(group):
+        a = pltpu.roll(own[0:mask_row], LANES - q * half, 1) if q else own[0:mask_row]
+        b = pltpu.roll(got[0:mask_row], (LANES - (q - 1) * half) % LANES, 1) if q != 1 else got[0:mask_row]
+        w = jnp.where(first_half, a, jnp.where(second_half, b, 0.0))
+        xj[pl.ds(q, wr, stride=group), :] = w[0:wr]
+    for j in range(R):
+        gd[1, j * hop : (j + 1) * hop, 0:LANES] = xj[j * hop : (j + 1) * hop]
+    for j in range(R):
+        xj[pl.ds(j, hop, stride=R), :] = gd[1, j * hop : (j + 1) * hop, 0:LANES]
 
     def head_pre(r):
         x = stream[pl.ds(r, cr)]
         f = x * (0.5 * jnp.tanh(0.5 * x) + 0.5)
         f = jnp.where(lane == C, 1.0, f).astype(BF16)
         feats[pl.ds(r, cr)] = f
-        pre[pl.ds(r, cr)] = dot(f[:, 0:C], mask_ref[...]) + mask_bias_ref[...]
+        pre[pl.ds(r, cr)] = dot(f[:, 0:C], mask_ref[...]) + mask_bias
 
     chunks(rows, cr, head_pre)
 
     hr = frames // 5
-    del seg_a, seg_b
 
     def tile(v):
         return jnp.broadcast_to(v[None], (hr // R, R, LANES)).reshape(hr, LANES)
@@ -330,13 +385,37 @@
     gd[1, R:frames, 0:LANES] = gd[0, R:frames, 0:LANES] + gd[0, 0 : frames - R, LANES : 2 * LANES]
     xj[frames : 2 * frames] = gd[1, 0:frames, 0:LANES]
     for j in range(R):
-        wave_out[j * hop : (j + 1) * hop] = xj[pl.ds(frames + j, hop, stride=R), :][:, 0 : 2 * half]
+        gd[1, j * hop : (j + 1) * hop, 0:LANES] = xj[pl.ds(frames + j, hop, stride=R), :]
+    xj[frames : 2 * frames] = gd[1, 0:frames, 0:LANES]
+    zero = jnp.zeros((wr, LANES), F32)
+    w_own, w_far = zero, zero
+    for q in range(group):
+        x = xj[pl.ds(frames + q, wr, stride=group), :]
+        a = jnp.where(first_half, x, 0.0)
+        b = jnp.where(second_half, x, 0.0)
+        w_own = w_own + (pltpu.roll(a, q * half, 1) if q else a)
+        w_far = w_far + (pltpu.roll(b, (q - 1) * half % LANES, 1) if q != 1 else b)
+    own[0:wr] = w_own
+    send[0:wr] = w_far
+    wave_swap = pltpu.make_async_remote_copy(
+        src_ref=send.at[0:mask_row],
+        dst_ref=wave_got,
+        send_sem=sems.at[2],
+        recv_sem=sems.at[3],
+        device_id=partner,
+        device_id_type=MESH,
+    )
+    wave_swap.start()
 
     gd[0, 0:frames, 0:LANES] = xj[0:frames]
     gd[0, 0 : frames - R, LANES : 2 * LANES] = xj[R:frames]
     gd[0, frames - R : frames, LANES : 2 * LANES] = next_not_first * xj[1 : R + 1]
     dp[0, 0:frames, 0 : 2 * LANES] = gd[0, 0:frames, 0 : 2 * LANES].astype(BF16)
-    dec_out[...] = dot_tn(masked[...], dp[0, 0:frames, 0 : 2 * LANES])
+    g = dot_tn(masked[...], dp[0, 0:frames, 0 : 2 * LANES])
+    g_lead = g[0:C, 0:LANES] + pltpu.roll(g[C : 2 * C, 0:LANES], LANES - half, 1)
+    g_tail = pltpu.roll(g[0:C, LANES : 2 * LANES], half, 1) + g[C : 2 * C, LANES : 2 * LANES]
+    g = jnp.where(first_half, g_lead, g_tail)
+    dec_out[...] = jnp.concatenate([g, jnp.zeros_like(g)], axis=0).T[0 : 2 * half, 0:C]
     xj[frames : frames + 8] = jnp.zeros((8, LANES), F32)
     for q in range(5):
         r = q * hr
@@ -347,8 +426,11 @@
         r = q * hr
         dpre[frames + r : frames + r + hr] = (tile(next_not_first) * xj[r + 1 : r + 1 + hr]).astype(BF16)
     gm = dot_tn(feats[...], dpre[...])
-    mask_out[...] = gm[0:C]
-    mask_bias_out[...] = gm[C : C + 1]
+    far = pltpu.roll(gm, C, 1)
+    mask_out[speaker] = gm[0:C, 0:C]
+    mask_out[1 - speaker] = far[0:C, 0:C]
+    mask_bias_out[speaker] = gm[C : C + 1, 0:C]
+    mask_bias_out[1 - speaker] = far[C : C + 1, 0:C]
     dz[...] = jnp.zeros_like(dz)
 
     def head_dz(r):
@@ -412,10 +494,10 @@
     def run_backward(b, sec, u, hc, sv, n, steps, unroll):
         total = n * steps
         size = total // 4
-        proj_out[b, sec] = dot_tn(dmj[0:total], hc[b]).T[:, 0:C]
+        proj_out[b, sec] = dot_tn(dmj[0:total], hc[b])[0:C]
 
         def joined(r):
-            dh[pl.ds(r, size)] = dot_nt(dmj[pl.ds(r, size)], pws[b, sec])
+            dh[pl.ds(r, size)] = dot(dmj[pl.ds(r, size)], pws[b, sec])
 
         chunks(total, size, joined)
         for d in range(2):
@@ -488,7 +570,13 @@
 
     chunks(rows, cr, finish)
     for j in range(R):
-        spans_out[j] = dz[pl.ds(j, K, stride=R), :][:, 0:C]
+        spans_out[j] = dz[pl.ds(j, K, stride=R), :].T[0:C]
+    wave_swap.wait()
+    for i in range(wr):
+        at = pl.multiple_of(speaker * (wr * LANES) + i * LANES, LANES)
+        wave_out[0:1, pl.ds(at, LANES)] = own[i : i + 1]
+        at = pl.multiple_of((1 - speaker) * (wr * LANES) + i * LANES, LANES)
+        wave_out[0:1, pl.ds(at, LANES)] = wave_got[i : i + 1]
 
 
 def shards(
@@ -515,30 +603,10 @@
     clips = clip_lengths.shape[2]
     frames = encoded.shape[0]
     half = dec_weight.shape[1] // 2
-    samples = frames * half
     kp = -(-K // 16) * 16
     rows, rows_e = R * K, R * kp
-
-    mine = lax.dynamic_slice_in_dim(wave_grad[0], speaker * samples, samples, 0)
-    theirs = lax.dynamic_slice_in_dim(wave_grad[0], (1 - speaker) * samples, samples, 0)
-    sent = jnp.concatenate([theirs, mask_weight.reshape(-1), mask_bias.reshape(-1)])
-    got = lax.ppermute(sent, "spk", [(0, 1), (1, 0)])
-    other_mask = got[samples : samples + C * C].reshape(C, C)
-    other_bias = got[samples + C * C :].reshape(1, C)
-    dw = jnp.concatenate([mine.reshape(frames, half), got[:samples].reshape(frames, half)], axis=1)
-    dw = jnp.pad(dw.astype(F32), ((0, 0), (0, LANES - 2 * half)))
-    masks = jnp.concatenate([mask_weight[0], other_mask], axis=1)
-    mask_biases = jnp.concatenate([mask_bias, other_bias], axis=1).astype(F32)
-    zero = jnp.zeros((C, half), BF16)
-    pad = jnp.zeros((C, LANES - 2 * half), BF16)
-    lead, tail = dec_weight[:, :half], dec_weight[:, half:]
-    dec = jnp.concatenate(
-        [
-            jnp.concatenate([lead, zero, pad, tail, zero, pad], axis=1),
-            jnp.concatenate([zero, lead, pad, zero, tail, pad], axis=1),
-        ],
-        axis=0,
-    )
+    wr = frames * half // LANES
+    mask_row = -(-wr // 8) * 8
 
     sizes = (R, K, C, H, clips, blocks, kp)
     smem = pl.BlockSpec(memory_space=pltpu.SMEM)
@@ -547,18 +615,18 @@
     outs = pl.pallas_call(
         functools.partial(local_kernel, sizes),
         out_shape=(
-            shape((frames, 2 * half), F32),
-            shape((R, K, C), F32),
+            shape((1, 2 * frames * half), F32),
+            shape((R, C, K), F32),
             shape((blocks, 2, 2, C, 4 * H), F32),
             shape((blocks, 2, 2, H, 4 * H), F32),
             shape((blocks, 2, 2, 4 * H), F32),
-            shape((blocks, 2, 2 * H, C), F32),
+            shape((blocks, 2, C, 2 * H), F32),
             shape((blocks, 2, C), F32),
             shape((blocks, 2, C), F32),
             shape((blocks, 2, C), F32),
-            shape((C, 2 * C), F32),
-            shape((1, 2 * C), F32),
-            shape((2 * C, 2 * LANES), F32),
+            shape((2, C, C), F32),
+            shape((2, 1, C), F32),
+            shape((2 * half, C), F32),
         ),
         in_specs=[smem, smem] + [vmem] * 13,
         out_specs=tuple([vmem] * 12),
@@ -584,66 +652,56 @@
             pltpu.VMEM((2, H, 4 * H), BF16),
             pltpu.VMEM((LANES, 8 * H), BF16),
             pltpu.VMEM((2, 4 * H, H), BF16),
-            pltpu.VMEM((blocks, 2, 2 * H, LANES), BF16),
+            pltpu.VMEM((blocks, 2, LANES, 2 * H), BF16),
             pltpu.VMEM((2 * blocks, 8, LANES), F32),
             pltpu.VMEM((frames, LANES), F32),
             pltpu.VMEM((rows, LANES), F32),
             pltpu.VMEM((frames, LANES), BF16),
             pltpu.VMEM((rows, LANES), BF16),
             pltpu.VMEM((rows, LANES), BF16),
+            pltpu.VMEM((C, 2 * C), BF16),
+            pltpu.VMEM((2 * C, 2 * LANES), BF16),
+            pltpu.VMEM((mask_row + C + 8, LANES), F32),
+            pltpu.VMEM((mask_row, LANES), F32),
+            pltpu.VMEM((mask_row + C + 8, LANES), F32),
+            pltpu.VMEM((mask_row, LANES), F32),
+            pltpu.SemaphoreType.DMA((4,)),
         ],
-        compiler_params=pltpu.CompilerParams(vmem_limit_bytes=62 * 1024 * 1024),
+        compiler_params=pltpu.CompilerParams(
+            vmem_limit_bytes=62 * 1024 * 1024, collective_id=0, has_side_effects=True
+        ),
         name="dual_path",
     )(
         clip_lengths,
         clip_pads,
-        spans,
-        encoded,
+        spans.transpose(0, 2, 1),
+        encoded.T,
         lstm_in,
         lstm_rec,
         lstm_bias,
-        proj_weight,
+        proj_weight.transpose(0, 1, 3, 2),
         proj_bias,
         gln_gain,
         gln_shift,
-        masks,
-        mask_biases,
-        dec,
-        dw,
+        mask_weight,
+        mask_bias,
+        dec_weight.T,
+        wave_grad,
     )
-    wave, grad_spans = outs[0], outs[1]
-    own_wave = wave[:, :half].reshape(-1)
-    far_wave = lax.ppermute(wave[:, half:].reshape(-1), "spk", [(0, 1), (1, 0)])
-    first = speaker == 0
-    waveforms = jnp.where(
-        first,
-        jnp.concatenate([own_wave, far_wave]),
-        jnp.concatenate([far_wave, own_wave]),
-    )[None]
-
-    def by_speaker(x):
-        a, b = x[:, :C], x[:, C:]
-        return jnp.where(first, jnp.stack([a, b]), jnp.stack([b, a]))
-
-    gd = outs[11]
-    grad_dec = jnp.concatenate(
-        [
-            gd[:C, :half] + gd[C:, half : 2 * half],
-            gd[:C, LANES : LANES + half] + gd[C:, LANES + half : LANES + 2 * half],
-        ],
-        axis=1,
-    )
-    summed = lax.psum(
-        outs[2:9] + (by_speaker(outs[9]), by_speaker(outs[10])[:, 0], grad_dec), ("dp", "spk")
-    )
+    summed = lax.psum(outs[2:], ("dp", "spk"))
     return (
-        (waveforms, grad_spans)
-        + summed[:7]
-        + (
-            lax.dynamic_slice_in_dim(summed[7], speaker, 1, 0),
-            lax.dynamic_slice_in_dim(summed[8], speaker, 1, 0),
-            summed[9],
-        )
+        outs[0],
+        outs[1].transpose(0, 2, 1),
+        summed[0],
+        summed[1],
+        summed[2],
+        summed[3].transpose(0, 1, 3, 2),
+        summed[4],
+        summed[5],
+        summed[6],
+        lax.dynamic_slice_in_dim(summed[7], speaker, 1, 0),
+        lax.dynamic_slice_in_dim(summed[8][:, 0], speaker, 1, 0),
+        summed[9].T,
     )
 
 

time: 297 us -> 280 us (0.943)
  local copies, waits for them, and re-layouts: 19.2 us -> 7.59 us
  other arithmetic: 4.22 us -> 0 us
  starting transfers between devices: 3.08 us -> 0.04 us
  Pallas kernels: 116 us -> 119 us
    unnamed x31 -> x27, local copies, waits for them, and re-layouts: 12.7 us -> 6.46 us
    ppermute x2 -> x0, starting transfers between devices: 3.04 us -> none  [the longest x1 2.97 us: shards(): got = lax.ppermute(sent, 'spk', [(0, 1), (1, 0)])]
  transfers between devices with their start and end apart: 3 -> 1, of which waited for: 1 -> 1; matrix products, arithmetic and copies ran while one was open for 4% -> 0% of each run, Pallas kernels for 0% -> 0%
where the time goes in v1:
time: 280 us
  Pallas kernels  119 us (42%)
  waiting for transfers between devices  97.2 us (35%)
  blocking collectives  41.7 us (15%)
  between operations  14.2 us (5%)
  local copies, waits for them, and re-layouts  7.59 us (3%)
    pallas_call x1, Pallas kernels, shards(): pl.pallas_call(functools.partial(local_kernel, sizes), out_shape=(shape((...  119 us
    psum x1, waiting for transfers between devices, shards(): summed = lax.psum(outs[2:], ('dp', 'spk'))  97.2 us
    psum x1, blocking collectives, shards(): summed = lax.psum(outs[2:], ('dp', 'spk'))  41.7 us
    unnamed x27, local copies, waits for them, and re-layouts  6.46 us
  transfers between devices with their start and end apart: 1, of which 1 were waited for; matrix products, arithmetic and copies ran while one was open for 0% of the time, Pallas kernels for 0%

profile of v1, /device:TPU:0, one launch (start us, length us, event | category | flops | bytes accessed | tf_op | source)
XLA Modules:
  0.0 279.8 jit_solution(17494164073370175467)
XLA Ops:
  7.2 0.0 all-reduce.4.cloned.1.call-start
  7.2 119.2 %dual_path.1 = (f32[1,12800]{1,0:T(1,128)}, f32[16,64,100]{2,1,0:T(8,128)}, f32[2,2,2,64,512]{4,3,2,1,0:T(8,128)}, f32[2,2,2,128,512]{4,3,2,1,0:T(8,128)}, f32[2...) custom-call(s32[1,2,3]{2,1,0:T(2,128)} %lengths_ref.1, ...), custom_call_target="tpu_custom_call" | custom-call | tf_op jit(solution)/shard_map/dual_path/pallas_call | solution.py:615
  126.4 0.0 copy-start.3
  126.4 0.0 copy-start.5
  126.4 0.0 copy-start.6
  126.4 0.0 copy-start.7
  126.4 0.0 copy-start.8
  126.4 0.0 copy-start.9
  126.5 0.0 copy-start.10
  126.5 0.0 copy-start.4
  126.5 0.0 copy-start.1
  126.5 0.0 all-reduce.4.cloned.1.call-update
  126.5 0.7 copy-done.3
  127.2 0.0 copy-done.5
  127.2 0.0 copy-done.6
  127.2 0.0 copy-done.7
  127.2 0.0 copy-done.8
  127.2 0.0 copy-done.9
  127.3 0.0 copy-done.10
  127.3 41.7 %all-reduce = (f32[2,2,2,512]{3,2,1,0:T(2,128)}, f32[2,2,64]{2,1,0:T(2,128)}, f32[2,2,64]{2,1,0:T(2,128)}, f32[2,2,64]{2,1,0:T(2,128)}, f32[2,64,64]{2,1,0:T(8,1...) all-reduce(f32[2,2,2,512]{3,2,1,0:T(2,128)S(1)} %copy-done.5, ...), channel_id=1, replica_groups=mesh['dp'=16,'spk'=2] {'dp','spk'}, use_global_device_ids=true, to_apply=%region_2.0 | all-reduce | flops 14208 | bytes 113664 | tf_op jit(solution)/shard_map/psum | solution.py:691
  169.0 0.5 dynamic-slice_bitcast_fusion
  169.5 0.6 constant_dynamic-slice_fusion
  170.1 97.2 %all-reduce.4.cloned.1.call-done = (f32[2,2,2,64,512]{4,3,2,1,0:T(8,128)}, f32[2,2,2,128,512]{4,3,2,1,0:T(8,128)}, f32[2,2,256,64]{2,3,1,0:T(8,128)}) async-done(((f32[2,2,2,64,512]{4,3,2,1,0:T(8,128)}, f32[2,2,2,128,512]{4,3,2,1,0:T(8,128)}, f32[2,2,256,64]{2,3,1,0:T(8,128)}), (f32[2,2,2,64,512]{4,3,2,1,0:T(8,128)}, f32[2,2,2,128,512]{4,3,2,1,0:T(8,128)}, ...) | async-done | bytes 3407888 | tf_op jit(solution)/shard_map/psum | solution.py:691
  267.3 0.0 copy-done.4
  267.3 0.6 copy.35
  267.9 0.0 copy-done.1
  267.9 0.8 copy.36
  268.7 2.3 copy.37
  271.0 0.0 copy-done
  271.0 1.3 copy.38
  272.3 0.0 copy-done.2
  272.3 0.7 copy.39
  (2 shorter events, 0.0 us)
Async XLA Ops:
  7.2 260.1 %all-reduce.4.cloned.1.call-start = ((), (), s32[]{:S(2)}) async-start(), calls=%async_computation | async-start | bytes 6815744 | tf_op jit(solution)/shard_map/psum | solution.py:691
  126.4 0.8 copy-start.3
  126.4 0.8 copy-start.5
  126.4 0.8 copy-start.6
  126.4 0.8 copy-start.7
  126.4 0.8 copy-start.8
  126.4 0.8 copy-start.9
  126.5 0.8 copy-start.10
  126.5 140.8 %copy-start.4 = (f32[1,12800]{1,0:T(1,128)S(1)}, f32[1,12800]{1,0:T(1,128)}, u32[]{:S(2)}) copy-start(f32[1,12800]{1,0:T(1,128)} %get-tuple-element.58) | copy-start | bytes 153604
  126.5 141.4 %copy-start.1 = (f32[16,64,100]{2,1,0:T(8,128)S(1)}, f32[16,64,100]{2,1,0:T(8,128)}, u32[]{:S(2)}) copy-start(f32[16,64,100]{2,1,0:T(8,128)} %get-tuple-element.25) | copy-start | bytes 1228804
  267.3 3.7 %copy-start = (f32[2,2,2,128,512]{4,3,2,1,0:T(8,128)S(1)}, f32[2,2,2,128,512]{4,3,2,1,0:T(8,128)}, u32[]{:S(2)}) copy-start(f32[2,2,2,128,512]{4,3,2,1,0:T(8,128)} %get-tuple-element.61) | copy-start | bytes 6291460
  271.0 1.3 copy-start.2
Sparse Core Ops, SparseCore 0:
  126.6 140.6 all-reduce.3

commit v2 on v1

--- a/solution.py
+++ b/solution.py
@@ -10,6 +10,7 @@
 F32 = jnp.float32
 BF16 = jnp.bfloat16
 LANES = 128
+PART = 16
 MESH = pl.DeviceIdType.MESH
 
 
@@ -33,6 +34,101 @@
         return carry
 
     lax.fori_loop(0, total // size, step, 0)
+
+
+class Butterfly:
+    def __init__(self, buf, recv, out, sems, hops):
+        self.buf, self.recv, self.out, self.sems = buf, recv, out, sems
+        self.steps = []
+        size, off, at = buf.shape[0], 0, 0
+        back = []
+        for p, (bit, partner) in enumerate(hops):
+            if size > PART:
+                size //= 2
+                keep, give = off + bit * size, off + (1 - bit) * size
+                back.append((p, keep, size, partner))
+            else:
+                keep = give = off
+            self.steps.append((self.give, self.take, (p, give, keep, at, size, partner)))
+            off = keep
+            at += size
+        self.part = off, size
+        self.last = len(self.steps)
+        for p, keep, size, partner in reversed(back):
+            self.steps.append((self.spread, None, (len(hops) + p, keep, size, partner)))
+        self.pending = None
+        self.done = 0
+
+    def copy(self, p, src, dst, partner):
+        return pltpu.make_async_remote_copy(
+            src_ref=src,
+            dst_ref=dst,
+            send_sem=self.sems.at[p, 0],
+            recv_sem=self.sems.at[p, 1],
+            device_id=partner,
+            device_id_type=MESH,
+        )
+
+    def give(self, p, give, keep, at, size, partner):
+        rows = self.buf.at[pl.ds(pl.multiple_of(give, PART), size)]
+        return self.copy(p, rows, self.recv.at[at : at + size], partner)
+
+    def take(self, p, give, keep, at, size, partner):
+        def add(i, carry):
+            own = pl.ds(pl.multiple_of(keep + i * PART, PART), PART)
+            new = self.recv[pl.ds(pl.multiple_of(at + i * PART, PART), PART)]
+            self.buf[own] = (self.buf[own].astype(F32) + new.astype(F32)).astype(BF16)
+            return carry
+
+        lax.fori_loop(0, size // PART, add, 0)
+
+    def spread(self, p, keep, size, partner):
+        rows = self.out.at[pl.ds(pl.multiple_of(keep, PART), size)]
+        return self.copy(p, rows, rows, partner)
+
+    def advance(self):
+        if self.pending is not None:
+            copy, after, what = self.pending
+            copy.wait()
+            if after is not None:
+                after(*what)
+            self.pending = None
+        if self.done == self.last:
+            off, size = self.part
+            rows = pl.ds(pl.multiple_of(off, PART), size)
+            self.out[rows] = self.buf[rows]
+        if self.done < len(self.steps):
+            start, after, what = self.steps[self.done]
+            copy = start(*what)
+            copy.start()
+            self.pending = (copy, after, what)
+            self.done += 1
+
+    def over(self):
+        return self.pending is None and self.done == len(self.steps)
+
+
+def hops_of(num_dp):
+    dp, spk = lax.axis_index("dp"), lax.axis_index("spk")
+    bits = num_dp.bit_length() - 1
+
+    def bit(k):
+        return dp // (1 << k) % 2
+
+    def flip(k, amount=1):
+        return dp + amount * (1 - 2 * bit(k)) * (1 << k)
+
+    def along_dp(k):
+        return bit(k), {"dp": flip(k), "spk": spk}
+
+    hops = [along_dp(0)]
+    first = 1 - bit(0)
+    second = bit(0)
+    for a, b in ((first, second), (second, first)):
+        hops.append(
+            (a * bit(1) + b * spk, {"dp": flip(1, a), "spk": spk + b * (1 - 2 * spk)})
+        )
+    return hops + [along_dp(k) for k in range(2, bits)]
 
 
 def local_kernel(
@@ -54,16 +150,7 @@
     wave_grad_ref,
     wave_out,
     spans_out,
-    in_out,
-    rec_out,
-    bias_out,
-    proj_out,
-    proj_bias_out,
-    gain_out,
-    shift_out,
-    mask_out,
-    mask_bias_out,
-    dec_out,
+    all_sums,
     stream,
     valid,
     mx,
@@ -99,8 +186,12 @@
     got,
     wave_got,
     sems,
+    sums,
+    recv,
+    small,
+    sum_sems,
 ):
-    R, K, C, H, clips, blocks, kp = sizes
+    R, K, C, H, clips, blocks, kp, num_dp = sizes
     rows, rows_e = R * K, R * kp
     hop = K // 2
     frames = R * hop
@@ -112,7 +203,9 @@
     partner = {"spk": 1 - speaker}
 
     barrier = pltpu.get_barrier_semaphore()
-    pl.semaphore_signal(barrier, inc=1, device_id=partner, device_id_type=MESH)
+    hops = hops_of(num_dp)
+    for bit, device in hops:
+        pl.semaphore_signal(barrier, inc=1, device_id=device, device_id_type=MESH)
 
     mask_row = -(-wr // 8) * 8
     for i in range(wr):
@@ -126,7 +219,7 @@
     bias_f = mask_bias_in_ref[0:1].astype(F32)
     bias_f = jnp.concatenate([bias_f, bias_f], axis=1)
     send[mask_row + C : mask_row + C + 8] = jnp.broadcast_to(bias_f, (8, LANES))
-    pl.semaphore_wait(barrier, 1)
+    pl.semaphore_wait(barrier, len(hops))
     swap = pltpu.make_async_remote_copy(
         src_ref=send, dst_ref=got, send_sem=sems.at[0], recv_sem=sems.at[1], device_id=partner, device_id_type=MESH
     )
@@ -161,8 +254,8 @@
         member = jnp.logical_and(jio >= starts[c], jio < ends[c]).astype(F32)
         members.append(member)
         thr = jnp.where(jio == ends[c] - 1, K - pads[c], thr)
-        total = (C * (K * lens[c] - pads[c])).astype(F32)
-        inv_count = inv_count + member / jnp.full((R, LANES), total, F32)
+        count = (C * (K * lens[c] - pads[c])).astype(F32)
+        inv_count = inv_count + member / jnp.full((R, LANES), count, F32)
     not_first = 1.0 - is_start(jio).astype(F32)
     next_not_first = 1.0 - jnp.logical_or(is_start(jio + 1), jio == R - 1).astype(F32)
 
@@ -179,6 +272,17 @@
         valid[pl.ds(r, cr)] = ok.reshape(cr, LANES)
 
     chunks(rows, cr, fill_valid)
+
+    reduces = [Butterfly(sums.at[n], recv.at[n], all_sums.at[n], sum_sems.at[n], hops) for n in range(2 * blocks)]
+    lay = sum_rows(C, H)
+    active = []
+
+    def point():
+        for reduce in active:
+            reduce.advance()
+
+    for n in range(2 * blocks):
+        sums[n, lay["head"] :] = jnp.zeros((sums.shape[1] - lay["head"], 4 * H), BF16)
 
     pws[...] = jnp.zeros_like(pws)
     wis[...] = jnp.zeros_like(wis)
@@ -415,7 +519,7 @@
     g_lead = g[0:C, 0:LANES] + pltpu.roll(g[C : 2 * C, 0:LANES], LANES - half, 1)
     g_tail = pltpu.roll(g[0:C, LANES : 2 * LANES], half, 1) + g[C : 2 * C, LANES : 2 * LANES]
     g = jnp.where(first_half, g_lead, g_tail)
-    dec_out[...] = jnp.concatenate([g, jnp.zeros_like(g)], axis=0).T[0 : 2 * half, 0:C]
+    g_dec = jnp.concatenate([g, jnp.zeros_like(g)], axis=0).T[0 : 2 * half]
     xj[frames : frames + 8] = jnp.zeros((8, LANES), F32)
     for q in range(5):
         r = q * hr
@@ -426,11 +530,12 @@
         r = q * hr
         dpre[frames + r : frames + r + hr] = (tile(next_not_first) * xj[r + 1 : r + 1 + hr]).astype(BF16)
     gm = dot_tn(feats[...], dpre[...])
-    far = pltpu.roll(gm, C, 1)
-    mask_out[speaker] = gm[0:C, 0:C]
-    mask_out[1 - speaker] = far[0:C, 0:C]
-    mask_bias_out[speaker] = gm[C : C + 1, 0:C]
-    mask_bias_out[1 - speaker] = far[C : C + 1, 0:C]
+    gm = jnp.where(speaker == 0, gm, pltpu.roll(gm, C, 1))
+    n, at = 2 * blocks - 1, lay["head"]
+    for q in range(4):
+        sums[n, at : at + 16, q * LANES : (q + 1) * LANES] = gm[16 * q : 16 * q + 16].astype(BF16)
+    sums[n, at + 16 : at + 32, 0:LANES] = jnp.where(lane < C, g_dec, 0.0).astype(BF16)
+    sums[n, at + 16 : at + 32, LANES : 2 * LANES] = jnp.broadcast_to(gm[C : C + 1], (16, LANES)).astype(BF16)
     dz[...] = jnp.zeros_like(dz)
 
     def head_dz(r):
@@ -457,8 +562,8 @@
 
         zero = jnp.zeros((R, LANES), F32)
         s1, s2 = lax.fori_loop(0, rows // cr, sums, (zero, zero))
-        shift_out[b, sec : sec + 1] = jnp.sum(s1, axis=0, keepdims=True)[:, 0:C]
-        gain_out[b, sec : sec + 1] = jnp.sum(s2, axis=0, keepdims=True)[:, 0:C]
+        small[2:3, LANES : 2 * LANES] = jnp.sum(s2, axis=0, keepdims=True)
+        small[2:3, 2 * LANES : 3 * LANES] = jnp.sum(s1, axis=0, keepdims=True)
         m1 = clip_sum(s1 * gain) * inv_count
         m2 = clip_sum(s2 * gain) * inv_count
         inv = inv_all[n]
@@ -477,7 +582,7 @@
             return acc + jnp.sum(y.reshape(cr // R, R, LANES), axis=0)
 
         acc = lax.fori_loop(0, rows // cr, apply, zero)
-        proj_bias_out[b, sec : sec + 1] = jnp.sum(acc, axis=0, keepdims=True)[:, 0:C]
+        small[2:3, 0:LANES] = jnp.sum(acc, axis=0, keepdims=True)
 
     def back_step(d, sv, b, r, n, dhn, dcn, keep):
         a = [sv[b, d, pl.ds(r, n), m * H : (m + 1) * H].astype(F32) for m in range(6)]
@@ -491,10 +596,15 @@
             dhn, dcn = dhn * keep, dcn * keep
         return dhn, dcn
 
-    def run_backward(b, sec, u, hc, sv, n, steps, unroll):
+    def run_backward(b, sec, u, hc, sv, n, steps, unroll, parts):
         total = n * steps
         size = total // 4
-        proj_out[b, sec] = dot_tn(dmj[0:total], hc[b])[0:C]
+        out = sums.at[2 * b + sec]
+        g = dot_tn(dmj[0:total], hc[b])[0:C].astype(BF16)
+        at = lay["proj"]
+        out[at : at + C // 2, 0 : 2 * H] = g[0 : C // 2]
+        out[at : at + C // 2, 2 * H : 4 * H] = g[C // 2 : C]
+        point()
 
         def joined(r):
             dh[pl.ds(r, size)] = dot(dmj[pl.ds(r, size)], pws[b, sec])
@@ -518,7 +628,11 @@
             return hf, hb, cf, cb
 
         z = jnp.zeros((n, H), F32)
-        lax.fori_loop(0, steps, step, (z, z, z, z), unroll=unroll)
+        carry = (z, z, z, z)
+        point()
+        for p in range(parts):
+            carry = lax.fori_loop(p * steps // parts, (p + 1) * steps // parts, step, carry, unroll=unroll)
+            point()
         if sec == 1:
             for j in range(1, steps):
                 kf = (1.0 - is_start(j).astype(F32)).astype(BF16)
@@ -529,23 +643,27 @@
                 hc[b, at, H : 2 * H] = hc[b, at, H : 2 * H] * kb
         for d in range(2):
             g = dot_tn(u[b], dp[d, 0:total])
-            in_out[b, sec, d] = g[0:C]
-            bias_out[b, sec, d : d + 1] = g[C : C + 1]
-        rec_out[b, sec, 0] = dot_tn(hc[b, 0 : total - n, 0:H], dp[0, n:total])
-        rec_out[b, sec, 1] = dot_tn(hc[b, n:total, H : 2 * H], dp[1, 0 : total - n])
+            out[lay["in"] + d * C : lay["in"] + (d + 1) * C] = g[0:C].astype(BF16)
+            small[d : d + 1] = g[C : C + 1]
+        at = lay["rec"]
+        out[at : at + H] = dot_tn(hc[b, 0 : total - n, 0:H], dp[0, n:total]).astype(BF16)
+        out[at + H : at + 2 * H] = dot_tn(hc[b, n:total, H : 2 * H], dp[1, 0 : total - n]).astype(BF16)
+        out[lay["small"] : lay["small"] + 16] = small[...].astype(BF16)
+        active.append(reduces[2 * b + sec])
+        point()
 
     def stream_grad(r, size):
         return dot_nt(dp[0, pl.ds(r, size)], wiu[:, 0 : 4 * H]) + dot_nt(
             dp[1, pl.ds(r, size)], wiu[:, 4 * H : 8 * H]
         )
 
-    def backward_block(i, carry):
-        b = blocks - 1 - i
+    small[...] = jnp.zeros_like(small)
+    for b in reversed(range(blocks)):
         norm_backward(b, 1)
         mx[rows:rows_e] = jnp.zeros((rows_e - rows, LANES), F32)
         for j in range(R):
             dmj[pl.ds(j * kp, kp)] = mx[pl.ds(j, kp, stride=R), :].astype(BF16)
-        run_backward(b, 1, u_e, hc_e, sv_e, kp, R, 2)
+        run_backward(b, 1, u_e, hc_e, sv_e, kp, R, 2, 2)
 
         def grad_inter(r):
             xj[pl.ds(r, rows_e // 4)] = stream_grad(r, rows_e // 4)
@@ -555,15 +673,12 @@
             dz[pl.ds(j, kp, stride=R), :] += xj[pl.ds(j * kp, kp)]
 
         norm_backward(b, 0)
-        run_backward(b, 0, u_a, hc_a, sv_a, R, K, 4)
+        run_backward(b, 0, u_a, hc_a, sv_a, R, K, 5, 4)
 
         def grad_intra(r):
             dz[pl.ds(r, rows // 4)] += stream_grad(r, rows // 4)
 
         chunks(rows, rows // 4, grad_intra)
-        return carry
-
-    lax.fori_loop(0, blocks, backward_block, 0)
 
     def finish(r):
         dz[pl.ds(r, cr)] = dz[pl.ds(r, cr)] * valid[pl.ds(r, cr)]
@@ -571,6 +686,8 @@
     chunks(rows, cr, finish)
     for j in range(R):
         spans_out[j] = dz[pl.ds(j, K, stride=R), :].T[0:C]
+    while not all(reduce.over() for reduce in active):
+        point()
     wave_swap.wait()
     for i in range(wr):
         at = pl.multiple_of(speaker * (wr * LANES) + i * LANES, LANES)
@@ -579,7 +696,71 @@
         wave_out[0:1, pl.ds(at, LANES)] = wave_got[i : i + 1]
 
 
+def unpack_kernel(
+    sizes,
+    sums,
+    wave_in,
+    spans_in,
+    wave_out,
+    spans_out,
+    in_out,
+    rec_out,
+    bias_out,
+    proj_out,
+    proj_bias_out,
+    gain_out,
+    shift_out,
+    mask_out,
+    mask_bias_out,
+    dec_out,
+):
+    C, H = sizes
+    lay = sum_rows(C, H)
+    n = pl.program_id(0)
+    b, sec = n // 2, n % 2
+    speaker = lax.axis_index("spk")
+    spans_out[...] = spans_in[...]
+    for d in range(2):
+        in_out[d] = sums[lay["in"] + d * C : lay["in"] + (d + 1) * C].astype(F32)
+        rec_out[d] = sums[lay["rec"] + d * H : lay["rec"] + (d + 1) * H].astype(F32)
+    at = lay["proj"]
+    proj_out[0 : C // 2] = sums[at : at + C // 2, 0 : 2 * H].astype(F32)
+    proj_out[C // 2 : C] = sums[at : at + C // 2, 2 * H : 4 * H].astype(F32)
+    small = sums[lay["small"] : lay["small"] + 16].astype(F32)
+    bias_out[...] = small[0:2]
+    for m, out in enumerate((proj_bias_out, gain_out, shift_out)):
+        out[b, pl.ds(sec, 1)] = small[2:3, m * LANES : m * LANES + C]
+
+    @pl.when(n == 0)
+    def _():
+        wave_out[...] = wave_in[...]
+
+    @pl.when(n == pl.num_programs(0) - 1)
+    def _():
+        at = lay["head"]
+
+        def own(x):
+            return jnp.where(speaker == 0, x, pltpu.roll(x, C, 1))[:, 0:C]
+
+        for q in range(4):
+            x = sums[at : at + 16, q * LANES : (q + 1) * LANES].astype(F32)
+            mask_out[0, 16 * q : 16 * q + 16] = own(x)
+        x = sums[at + 16 : at + 32, 0 : 2 * LANES].astype(F32)
+        mask_bias_out[...] = own(x[:, LANES : 2 * LANES])[0:1]
+        dec_out[...] = x[:, 0:C]
+
+
+def sum_rows(C, H):
+    lay, at = {}, 0
+    for name, rows in (("in", 2 * C), ("rec", 2 * H), ("proj", C // 2), ("small", 16), ("head", 32)):
+        lay[name] = at
+        at += rows
+    lay["total"] = -(-at // (32 * PART)) * 32 * PART
+    return lay
+
+
 def shards(
+    num_dp,
     spans,
     encoded,
     clip_lengths,
@@ -596,7 +777,6 @@
     dec_weight,
     wave_grad,
 ):
-    speaker = lax.axis_index("spk")
     R, K, C = spans.shape
     H = lstm_rec.shape[3]
     blocks = lstm_in.shape[0]
@@ -608,7 +788,9 @@
     wr = frames * half // LANES
     mask_row = -(-wr // 8) * 8
 
-    sizes = (R, K, C, H, clips, blocks, kp)
+    sizes = (R, K, C, H, clips, blocks, kp, num_dp)
+    lay = sum_rows(C, H)
+    num_hops = num_dp.bit_length()
     smem = pl.BlockSpec(memory_space=pltpu.SMEM)
     vmem = pl.BlockSpec(memory_space=pltpu.VMEM)
     shape = jax.ShapeDtypeStruct
@@ -617,19 +799,10 @@
         out_shape=(
             shape((1, 2 * frames * half), F32),
             shape((R, C, K), F32),
-            shape((blocks, 2, 2, C, 4 * H), F32),
-            shape((blocks, 2, 2, H, 4 * H), F32),
-            shape((blocks, 2, 2, 4 * H), F32),
-            shape((blocks, 2, C, 2 * H), F32),
-            shape((blocks, 2, C), F32),
-            shape((blocks, 2, C), F32),
-            shape((blocks, 2, C), F32),
-            shape((2, C, C), F32),
-            shape((2, 1, C), F32),
-            shape((2 * half, C), F32),
+            shape((2 * blocks, lay["total"], 4 * H), BF16),
         ),
         in_specs=[smem, smem] + [vmem] * 13,
-        out_specs=tuple([vmem] * 12),
+        out_specs=tuple([vmem] * 3),
         scratch_shapes=[
             pltpu.VMEM((rows_e, LANES), F32),
             pltpu.VMEM((rows, LANES), F32),
@@ -666,6 +839,10 @@
             pltpu.VMEM((mask_row + C + 8, LANES), F32),
             pltpu.VMEM((mask_row, LANES), F32),
             pltpu.SemaphoreType.DMA((4,)),
+            pltpu.VMEM((2 * blocks, lay["total"], 4 * H), BF16),
+            pltpu.VMEM((2 * blocks, lay["total"] + PART * max(num_hops - 5, 0), 4 * H), BF16),
+            pltpu.VMEM((16, 4 * H), F32),
+            pltpu.SemaphoreType.DMA((2 * blocks, 2 * num_hops, 2)),
         ],
         compiler_params=pltpu.CompilerParams(
             vmem_limit_bytes=62 * 1024 * 1024, collective_id=0, has_side_effects=True
@@ -688,26 +865,73 @@
         dec_weight.T,
         wave_grad,
     )
-    summed = lax.psum(outs[2:], ("dp", "spk"))
+    half = dec_weight.shape[1] // 2
+    per_section = pl.BlockSpec((None, lay["total"], 4 * H), lambda n: (n, 0, 0))
+
+    def whole(*dims):
+        return pl.BlockSpec(dims, lambda n: (0,) * len(dims))
+
+    def section(*dims):
+        return pl.BlockSpec((None, None) + dims, lambda n: (n // 2, n % 2) + (0,) * len(dims))
+
+    finals = pl.pallas_call(
+        functools.partial(unpack_kernel, (C, H)),
+        grid=(2 * blocks,),
+        out_shape=(
+            shape((1, 2 * frames * half), F32),
+            shape((R, C, K), F32),
+            shape((blocks, 2, 2, C, 4 * H), F32),
+            shape((blocks, 2, 2, H, 4 * H), F32),
+            shape((blocks, 2, 2, 4 * H), F32),
+            shape((blocks, 2, C, 2 * H), F32),
+            shape((blocks, 2, C), F32),
+            shape((blocks, 2, C), F32),
+            shape((blocks, 2, C), F32),
+            shape((1, C, C), F32),
+            shape((1, C), F32),
+            shape((2 * half, C), F32),
+        ),
+        in_specs=[
+            per_section,
+            whole(1, 2 * frames * half),
+            pl.BlockSpec((R // (2 * blocks), C, K), lambda n: (n, 0, 0)),
+        ],
+        out_specs=(
+            whole(1, 2 * frames * half),
+            pl.BlockSpec((R // (2 * blocks), C, K), lambda n: (n, 0, 0)),
+            section(2, C, 4 * H),
+            section(2, H, 4 * H),
+            section(2, 4 * H),
+            section(C, 2 * H),
+            whole(blocks, 2, C),
+            whole(blocks, 2, C),
+            whole(blocks, 2, C),
+            whole(1, C, C),
+            whole(1, C),
+            whole(2 * half, C),
+        ),
+        compiler_params=pltpu.CompilerParams(vmem_limit_bytes=32 * 1024 * 1024),
+        name="unpack",
+    )(outs[2], outs[0], outs[1])
     return (
-        outs[0],
-        outs[1].transpose(0, 2, 1),
-        summed[0],
-        summed[1],
-        summed[2],
-        summed[3].transpose(0, 1, 3, 2),
-        summed[4],
-        summed[5],
-        summed[6],
-        lax.dynamic_slice_in_dim(summed[7], speaker, 1, 0),
-        lax.dynamic_slice_in_dim(summed[8][:, 0], speaker, 1, 0),
-        summed[9].T,
+        finals[0],
+        finals[1].transpose(0, 2, 1),
+        finals[2],
+        finals[3],
+        finals[4],
+        finals[5].transpose(0, 1, 3, 2),
+        finals[6],
+        finals[7],
+        finals[8],
+        finals[9],
+        finals[10],
+        finals[11].T,
     )
 
 
 def solution(mesh):
     return jax.shard_map(
-        shards,
+        functools.partial(shards, mesh.shape["dp"]),
         mesh=mesh,
         in_specs=(
             P(("dp", "spk"), None, None),

time: 280 us -> 184 us (0.66)
  waiting for transfers between devices: 97.2 us -> 0 us
  Pallas kernels: 119 us -> 179 us
  blocking collectives: 41.7 us -> 0 us
  between operations: 14.2 us -> 0.83 us
  local copies, waits for them, and re-layouts: 7.59 us -> 3.43 us
    psum x1 -> x0, waiting for transfers between devices: 97.2 us -> none  [shards(): summed = lax.psum(outs[2:], ('dp', 'spk'))]
    pallas_call x1, Pallas kernels: 119 us -> 177 us  [shards(): pl.pallas_call(functools.partial(local_kernel, sizes), out_shape=(shape((...]
    psum x1 -> x0, blocking collectives: 41.7 us -> none  [shards(): summed = lax.psum(outs[2:], ('dp', 'spk'))]
    unnamed x27 -> x6, local copies, waits for them, and re-layouts: 6.46 us -> 3.43 us
  transfers between devices with their start and end apart: 1 -> 0, of which waited for: 1 -> 0; matrix products, arithmetic and copies ran while one was open for 0% -> 0% of each run, Pallas kernels for 0% -> 0%
where the time goes in v2:
time: 184 us
  Pallas kernels  179 us (97%)
  local copies, waits for them, and re-layouts  3.43 us (2%)
    pallas_call x1, Pallas kernels, shards(): pl.pallas_call(functools.partial(local_kernel, sizes), out_shape=(shape((...  177 us

profile of v2, /device:TPU:0, one launch (start us, length us, event | category | flops | bytes accessed | tf_op | source)
XLA Modules:
  0.0 183.5 jit_solution(13930430887042884487)
XLA Ops:
  0.7 176.8 %dual_path.1 = (f32[1,12800]{1,0:T(1,128)}, f32[16,64,100]{2,1,0:T(8,128)}, bf16[4,512,512]{2,1,0:T(8,128)(2,1)}) custom-call(s32[1,2,3]{2,1,0:T(2,128)} %lengths_ref.1, s32[1,2,3]{2,1,0:T(2,128)} %pads_ref.1, bf16[16,64,100]{2,1,0:T(8,128)(2,1)} %bitcast.7, bf16[64,800]{1,0:T(8,128)(2,1)} %bitcast.9, bf16[2,2,2,64,512]{4,3,2,1,0:T(8,128)(2,1)} %w_in_ref.1, ...), custom_call_target="tpu_custom_call" | custom-call | tf_op jit(solution)/shard_map/dual_path/pallas_call | solution.py:797
  177.4 0.0 copy-start
  177.4 1.6 copy-done
  179.0 0.0 copy-start.1
  179.0 1.0 copy-done.1
  180.1 0.0 copy-start.2
  180.1 0.8 copy-done.2
  180.9 2.5 %unpack.1 = (f32[1,12800]{1,0:T(1,128)}, f32[16,64,100]{2,1,0:T(8,128)}, f32[2,2,2,64,512]{4,3,2,1,0:T(8,128)}, f32[2,2,2,128,512]{4,3,2,1,0:T(8,128)}, f32[2,2,...) custom-call(bf16[4,512,512]{2,1,0:T(8,128)(2,1)S(1)} %copy-done, ...), custom_call_target="tpu_custom_call" | custom-call | tf_op jit(solution)/shard_map/unpack/pallas_call | solution.py:877
Async XLA Ops:
  177.4 1.6 copy-start
  179.0 1.0 copy-start.1
  180.1 0.8 copy-start.2

commit v3 on v2

--- a/solution.py
+++ b/solution.py
@@ -11,6 +11,7 @@
 BF16 = jnp.bfloat16
 LANES = 128
 PART = 16
+PAIR = 2 * PART
 MESH = pl.DeviceIdType.MESH
 
 
@@ -36,99 +37,140 @@
     lax.fori_loop(0, total // size, step, 0)
 
 
-class Butterfly:
-    def __init__(self, buf, recv, out, sems, hops):
-        self.buf, self.recv, self.out, self.sems = buf, recv, out, sems
-        self.steps = []
-        size, off, at = buf.shape[0], 0, 0
-        back = []
-        for p, (bit, partner) in enumerate(hops):
-            if size > PART:
-                size //= 2
-                keep, give = off + bit * size, off + (1 - bit) * size
-                back.append((p, keep, size, partner))
-            else:
-                keep = give = off
-            self.steps.append((self.give, self.take, (p, give, keep, at, size, partner)))
-            off = keep
+class Place:
+    def __init__(self, num_dp):
+        self.dp, self.spk = lax.axis_index("dp"), lax.axis_index("spk")
+        self.bits = num_dp.bit_length()
+
+    def bit(self, k):
+        if k == 1:
+            return self.spk
+        return self.dp // (1 << max(k - 1, 0)) % 2
+
+    def device(self, mask):
+        dp, spk = self.dp, self.spk
+        for k in range(self.bits):
+            if mask >> k & 1:
+                if k == 1:
+                    spk = 1 - spk
+                else:
+                    dp = dp + (1 - 2 * self.bit(k)) * (1 << max(k - 1, 0))
+        return {"dp": dp, "spk": spk}
+
+    def index(self, bits, mask=0):
+        number = 0
+        for i, k in enumerate(bits):
+            one = 1 - self.bit(k) if mask >> k & 1 else self.bit(k)
+            number = number + one * (1 << i)
+        return number
+
+    def masks(self, bits):
+        found = []
+        for m in range((1 << len(bits)) - 1, 0, -1):
+            found.append(sum((m >> i & 1) << k for i, k in enumerate(bits)))
+        return found
+
+
+class Reduction:
+    def __init__(self, buf, recv, out, sems, place, stages, outer, times):
+        self.buf, self.recv, self.out, self.sems, self.place = buf, recv, out, sems, place
+        self.steps, back = [], []
+        off, size, at, sem = 0, buf.shape[0], 0, 0
+        for i, bits in enumerate(stages):
+            masks = place.masks(bits)
+            part = size // (len(masks) + 1)
+            own = off + place.index(bits) * part
+            last = i == len(stages) - 1
+            self.steps.append(
+                (
+                    functools.partial(self.scatter, sem, masks, bits, off, part, at),
+                    functools.partial(self.add, len(masks), own, part, at, out if last else buf),
+                    times[len(bits)],
+                )
+            )
+            back.append((masks, own, part, times[len(bits)]))
+            off, size = own, part
+            at += len(masks) * part
+            sem += 1
+        for k in outer:
+            self.steps.append(
+                (
+                    functools.partial(self.double, sem, k, off, size, at),
+                    functools.partial(self.add_double, off, size, at),
+                    times[1],
+                )
+            )
             at += size
-        self.part = off, size
-        self.last = len(self.steps)
-        for p, keep, size, partner in reversed(back):
-            self.steps.append((self.spread, None, (len(hops) + p, keep, size, partner)))
-        self.pending = None
-        self.done = 0
-
-    def copy(self, p, src, dst, partner):
+            sem += 1
+        for masks, own, part, time in reversed(back):
+            self.steps.append((functools.partial(self.gather, sem, masks, own, part), None, time))
+            sem += 1
+        self.first = self.steps[0][1]
+        self.pending, self.after, self.due = None, None, 0.0
+
+    def copy(self, sem, src, dst, device):
         return pltpu.make_async_remote_copy(
             src_ref=src,
             dst_ref=dst,
-            send_sem=self.sems.at[p, 0],
-            recv_sem=self.sems.at[p, 1],
-            device_id=partner,
+            send_sem=self.sems.at[sem, 0],
+            recv_sem=self.sems.at[sem, 1],
+            device_id=device,
             device_id_type=MESH,
         )
 
-    def give(self, p, give, keep, at, size, partner):
-        rows = self.buf.at[pl.ds(pl.multiple_of(give, PART), size)]
-        return self.copy(p, rows, self.recv.at[at : at + size], partner)
-
-    def take(self, p, give, keep, at, size, partner):
-        def add(i, carry):
-            own = pl.ds(pl.multiple_of(keep + i * PART, PART), PART)
-            new = self.recv[pl.ds(pl.multiple_of(at + i * PART, PART), PART)]
-            self.buf[own] = (self.buf[own].astype(F32) + new.astype(F32)).astype(BF16)
+    def rows(self, ref, off, size):
+        return ref.at[pl.ds(pl.multiple_of(off, PART), size)]
+
+    def all_of(self, sem, masks, part):
+        rows = self.recv.at[0 : len(masks) * part]
+        return self.copy(sem, rows, rows, self.place.device(masks[0]))
+
+    def scatter(self, sem, masks, bits, off, part, at):
+        for i, mask in enumerate(masks):
+            src = self.rows(self.buf, off + self.place.index(bits, mask) * part, part)
+            dst = self.recv.at[at + i * part : at + (i + 1) * part]
+            self.copy(sem, src, dst, self.place.device(mask)).start()
+        return self.all_of(sem, masks, part)
+
+    def add(self, number, own, part, at, target):
+        def body(i, carry):
+            rows = pl.ds(pl.multiple_of(own + i * PART, PART), PART)
+            total = self.buf[rows].astype(F32)
+            for q in range(number):
+                total = total + self.recv[pl.ds(pl.multiple_of(at + q * part + i * PART, PART), PART)].astype(F32)
+            target[rows] = total.astype(BF16)
             return carry
 
-        lax.fori_loop(0, size // PART, add, 0)
-
-    def spread(self, p, keep, size, partner):
-        rows = self.out.at[pl.ds(pl.multiple_of(keep, PART), size)]
-        return self.copy(p, rows, rows, partner)
-
-    def advance(self):
+        lax.fori_loop(0, part // PART, body, 0)
+
+    def double(self, sem, k, off, size, at):
+        copy = self.copy(sem, self.rows(self.out, off, size), self.recv.at[at : at + size], self.place.device(1 << k))
+        copy.start()
+        return copy
+
+    def add_double(self, off, size, at):
+        rows = pl.ds(pl.multiple_of(off, PART), size)
+        self.out[rows] = (self.out[rows].astype(F32) + self.recv[at : at + size].astype(F32)).astype(BF16)
+
+    def gather(self, sem, masks, own, part):
+        rows = self.rows(self.out, own, part)
+        for mask in masks:
+            self.copy(sem, rows, rows, self.place.device(mask)).start()
+        return self.all_of(sem, masks, part)
+
+    def advance(self, now):
         if self.pending is not None:
-            copy, after, what = self.pending
-            copy.wait()
-            if after is not None:
-                after(*what)
+            self.pending.wait()
+            if self.after is not None:
+                self.after()
             self.pending = None
-        if self.done == self.last:
-            off, size = self.part
-            rows = pl.ds(pl.multiple_of(off, PART), size)
-            self.out[rows] = self.buf[rows]
-        if self.done < len(self.steps):
-            start, after, what = self.steps[self.done]
-            copy = start(*what)
-            copy.start()
-            self.pending = (copy, after, what)
-            self.done += 1
+        if self.steps:
+            start, self.after, time = self.steps.pop(0)
+            self.pending = start()
+            self.due = now + time
 
     def over(self):
-        return self.pending is None and self.done == len(self.steps)
-
-
-def hops_of(num_dp):
-    dp, spk = lax.axis_index("dp"), lax.axis_index("spk")
-    bits = num_dp.bit_length() - 1
-
-    def bit(k):
-        return dp // (1 << k) % 2
-
-    def flip(k, amount=1):
-        return dp + amount * (1 - 2 * bit(k)) * (1 << k)
-
-    def along_dp(k):
-        return bit(k), {"dp": flip(k), "spk": spk}
-
-    hops = [along_dp(0)]
-    first = 1 - bit(0)
-    second = bit(0)
-    for a, b in ((first, second), (second, first)):
-        hops.append(
-            (a * bit(1) + b * spk, {"dp": flip(1, a), "spk": spk + b * (1 - 2 * spk)})
-        )
-    return hops + [along_dp(k) for k in range(2, bits)]
+        return self.pending is None and not self.steps
 
 
 def local_kernel(
@@ -168,8 +210,7 @@
     gd,
     dh,
     dp,
-    wis,
-    wrs,
+    wcat,
     wiu,
     wrt,
     pws,
@@ -198,14 +239,15 @@
     half = dec_in_ref.shape[0] // 2
     wr = frames * half // LANES
     group = LANES // half
-    cr = 10 * R
+    cr = rows
     speaker = lax.axis_index("spk")
     partner = {"spk": 1 - speaker}
 
     barrier = pltpu.get_barrier_semaphore()
-    hops = hops_of(num_dp)
-    for bit, device in hops:
-        pl.semaphore_signal(barrier, inc=1, device_id=device, device_id_type=MESH)
+    place = Place(num_dp)
+    everyone = place.masks(range(1, min(place.bits, 5))) + [1 << k for k in [0, *range(5, place.bits)]]
+    for mask in everyone:
+        pl.semaphore_signal(barrier, inc=1, device_id=place.device(mask), device_id_type=MESH)
 
     mask_row = -(-wr // 8) * 8
     for i in range(wr):
@@ -219,7 +261,7 @@
     bias_f = mask_bias_in_ref[0:1].astype(F32)
     bias_f = jnp.concatenate([bias_f, bias_f], axis=1)
     send[mask_row + C : mask_row + C + 8] = jnp.broadcast_to(bias_f, (8, LANES))
-    pl.semaphore_wait(barrier, len(hops))
+    pl.semaphore_wait(barrier, len(everyone))
     swap = pltpu.make_async_remote_copy(
         src_ref=send, dst_ref=got, send_sem=sems.at[0], recv_sem=sems.at[1], device_id=partner, device_id_type=MESH
     )
@@ -227,7 +269,7 @@
 
     jio = lax.broadcasted_iota(jnp.int32, (R, LANES), 0)
     lane = lax.broadcasted_iota(jnp.int32, (1, LANES), 1)
-    ones_lane = (lane == C).astype(F32)
+    ones_lanes = jnp.logical_and(lane >= C, lane < C + 3)
 
     lens = [lengths_ref[0, speaker, c] for c in range(clips)]
     pads = [pads_ref[0, speaker, c] for c in range(clips)]
@@ -273,19 +315,28 @@
 
     chunks(rows, cr, fill_valid)
 
-    reduces = [Butterfly(sums.at[n], recv.at[n], all_sums.at[n], sum_sems.at[n], hops) for n in range(2 * blocks)]
+    near, far = list(range(1, min(place.bits, 3))), list(range(3, min(place.bits, 5)))
+    outer = range(5, place.bits)
+    times = {1: 2.0, 2: 4.5, 4: 7.0}
+
+    def reduction(n, stages):
+        return Reduction(sums.at[n], recv.at[n], all_sums.at[n], sum_sems.at[n], place, stages, outer, times)
+
     lay = sum_rows(C, H)
     active = []
-
-    def point():
+    clock = [0.0]
+
+    def point(passed):
+        clock[0] += passed
         for reduce in active:
-            reduce.advance()
+            if not reduce.over() and reduce.due <= clock[0]:
+                reduce.advance(clock[0])
 
     for n in range(2 * blocks):
-        sums[n, lay["head"] :] = jnp.zeros((sums.shape[1] - lay["head"], 4 * H), BF16)
+        for at in (lay["proj"], lay["head"]):
+            sums[n, at : at + PAIR] = jnp.zeros((PAIR, 4 * H), BF16)
 
     pws[...] = jnp.zeros_like(pws)
-    wis[...] = jnp.zeros_like(wis)
     wiu[...] = jnp.zeros_like(wiu)
     vec[...] = jnp.zeros_like(vec)
     for b in range(blocks):
@@ -304,7 +355,7 @@
 
     def start_stream(r):
         x = stream[pl.ds(r, cr)] * valid[pl.ds(r, cr)]
-        stream[pl.ds(r, cr)] = jnp.where(lane == C, 1.0, x)
+        stream[pl.ds(r, cr)] = jnp.where(ones_lanes, 1.0, x)
 
     chunks(rows, cr, start_stream)
 
@@ -316,7 +367,7 @@
         return x[:, g * H : (g + 1) * H]
 
     def gate_step(d, sv, b, r, n, p, c, keep_next):
-        acts = [jnp.tanh(p[:, g * H : (g + 1) * H] + gd[d, pl.ds(r, n), g * H : (g + 1) * H]) for g in range(4)]
+        acts = [jnp.tanh(p[:, g * H : (g + 1) * H]) for g in range(4)]
         ti, tf, g, to = acts
         i, f, o = 0.5 * ti + 0.5, 0.5 * tf + 0.5, 0.5 * to + 0.5
         cn = f * c + i * g
@@ -339,19 +390,18 @@
     def run_forward(b, sec, u, hc, sv, n, steps, unroll):
         total = n * steps
         for d in range(2):
-            w = w_in_ref[b, sec, d].astype(F32) * gate_scale
-            wis[0:C, d * 4 * H : (d + 1) * 4 * H] = w.astype(BF16)
-            wrs[d] = (w_rec_ref[b, sec, d].astype(F32) * gate_scale).astype(BF16)
-        size = total // 4
-
-        def drive(r):
-            for d in range(2):
-                bias = w_bias_ref[b, sec, d : d + 1] * gate_scale
-                gd[d, pl.ds(r, size)] = (
-                    dot(u[b, pl.ds(r, size)], wis[:, d * 4 * H : (d + 1) * 4 * H]) + bias
-                )
-
-        chunks(total, size, drive)
+            wcat[d, 0:H] = (w_rec_ref[b, sec, d].astype(F32) * gate_scale).astype(BF16)
+            wcat[d, H : H + C] = (w_in_ref[b, sec, d].astype(F32) * gate_scale).astype(BF16)
+            bias = w_bias_ref[b, sec, d : d + 1] * gate_scale
+            terms = []
+            for _ in range(3):
+                terms.append(bias.astype(BF16).astype(F32))
+                bias = bias - terms[-1]
+            row = lax.broadcasted_iota(jnp.int32, (H - C, 4 * H), 0)
+            block = jnp.zeros((H - C, 4 * H), F32)
+            for m, term in enumerate(terms):
+                block = jnp.where(row == m, jnp.broadcast_to(term, block.shape), block)
+            wcat[d, H + C : 2 * H] = block.astype(BF16)
 
         def step(t, carry):
             hf, hb, cf, cb = carry
@@ -362,8 +412,8 @@
             if sec == 1:
                 kf = 1.0 - is_start(t + 1).astype(F32)
                 kb = 1.0 - is_end(back - 1).astype(F32)
-            pf = dot(hf, wrs[0])
-            pb = dot(hb, wrs[1])
+            pf = dot(jnp.concatenate([hf, u[b, pl.ds(rf, n)]], axis=1), wcat[0])
+            pb = dot(jnp.concatenate([hb, u[b, pl.ds(rb, n)]], axis=1), wcat[1])
             out_f, hf, cf = gate_step(0, sv, b, rf, n, pf, cf, kf)
             out_b, hb, cb = gate_step(1, sv, b, rb, n, pb, cb, kb)
             hc[b, pl.ds(rf, n), 0:H] = out_f
@@ -405,24 +455,16 @@
             u_a[b, pl.ds(r, cr)] = stream[pl.ds(r, cr)].astype(BF16)
 
         chunks(rows, cr, u_intra)
-        run_forward(b, 0, u_a, hc_a, sv_a, R, K, 4)
-
-        def mix_intra(r):
-            mx[pl.ds(r, rows // 4)] = dot_nt(hc_a[b, pl.ds(r, rows // 4)], pws[b, 0]) + vec[2 * b, 0:1]
-
-        chunks(rows, rows // 4, mix_intra)
+        run_forward(b, 0, u_a, hc_a, sv_a, R, K, 10)
+
+        mx[0:rows] = dot_nt(hc_a[b], pws[b, 0]) + vec[2 * b, 0:1]
         norm_forward(b, 0)
 
         for j in range(R):
             u_e[b, pl.ds(j * kp, kp)] = stream[pl.ds(j, kp, stride=R), :].astype(BF16)
-        run_forward(b, 1, u_e, hc_e, sv_e, kp, R, 2)
-
-        def mix_inter(r):
-            xj[pl.ds(r, rows_e // 4)] = (
-                dot_nt(hc_e[b, pl.ds(r, rows_e // 4)], pws[b, 1]) + vec[2 * b + 1, 0:1]
-            )
-
-        chunks(rows_e, rows_e // 4, mix_inter)
+        run_forward(b, 1, u_e, hc_e, sv_e, kp, R, R)
+
+        xj[...] = dot_nt(hc_e[b], pws[b, 1]) + vec[2 * b + 1, 0:1]
         for j in range(R):
             mx[pl.ds(j, kp, stride=R), :] = xj[pl.ds(j * kp, kp)]
         norm_forward(b, 1)
@@ -562,8 +604,8 @@
 
         zero = jnp.zeros((R, LANES), F32)
         s1, s2 = lax.fori_loop(0, rows // cr, sums, (zero, zero))
-        small[2:3, LANES : 2 * LANES] = jnp.sum(s2, axis=0, keepdims=True)
-        small[2:3, 2 * LANES : 3 * LANES] = jnp.sum(s1, axis=0, keepdims=True)
+        small[1:2, LANES : 2 * LANES] = jnp.sum(s2, axis=0, keepdims=True)
+        small[1:2, 2 * LANES : 3 * LANES] = jnp.sum(s1, axis=0, keepdims=True)
         m1 = clip_sum(s1 * gain) * inv_count
         m2 = clip_sum(s2 * gain) * inv_count
         inv = inv_all[n]
@@ -582,7 +624,7 @@
             return acc + jnp.sum(y.reshape(cr // R, R, LANES), axis=0)
 
         acc = lax.fori_loop(0, rows // cr, apply, zero)
-        small[2:3, 0:LANES] = jnp.sum(acc, axis=0, keepdims=True)
+        small[1:2, 0:LANES] = jnp.sum(acc, axis=0, keepdims=True)
 
     def back_step(d, sv, b, r, n, dhn, dcn, keep):
         a = [sv[b, d, pl.ds(r, n), m * H : (m + 1) * H].astype(F32) for m in range(6)]
@@ -598,18 +640,13 @@
 
     def run_backward(b, sec, u, hc, sv, n, steps, unroll, parts):
         total = n * steps
-        size = total // 4
         out = sums.at[2 * b + sec]
         g = dot_tn(dmj[0:total], hc[b])[0:C].astype(BF16)
         at = lay["proj"]
         out[at : at + C // 2, 0 : 2 * H] = g[0 : C // 2]
         out[at : at + C // 2, 2 * H : 4 * H] = g[C // 2 : C]
-        point()
-
-        def joined(r):
-            dh[pl.ds(r, size)] = dot(dmj[pl.ds(r, size)], pws[b, sec])
-
-        chunks(total, size, joined)
+
+        dh[0:total] = dot(dmj[0:total], pws[b, sec])
         for d in range(2):
             wrt[d] = w_rec_ref[b, sec, d].T
             wiu[0:C, d * 4 * H : (d + 1) * 4 * H] = w_in_ref[b, sec, d]
@@ -629,10 +666,10 @@
 
         z = jnp.zeros((n, H), F32)
         carry = (z, z, z, z)
-        point()
+        point(2.5)
         for p in range(parts):
             carry = lax.fori_loop(p * steps // parts, (p + 1) * steps // parts, step, carry, unroll=unroll)
-            point()
+            point(steps * 0.125 / parts)
         if sec == 1:
             for j in range(1, steps):
                 kf = (1.0 - is_start(j).astype(F32)).astype(BF16)
@@ -641,21 +678,26 @@
                 kb = (1.0 - is_end(j - 1).astype(F32)).astype(BF16)
                 at = slice(j * n, (j + 1) * n)
                 hc[b, at, H : 2 * H] = hc[b, at, H : 2 * H] * kb
-        for d in range(2):
+        last = (b, sec) == (0, 0)
+        core = place.bit(0)
+        reduce = reduction(2 * b + sec, [[0], near + far] if last else [[0], near, far])
+        for d in (1 - core, core):
             g = dot_tn(u[b], dp[d, 0:total])
-            out[lay["in"] + d * C : lay["in"] + (d + 1) * C] = g[0:C].astype(BF16)
-            small[d : d + 1] = g[C : C + 1]
-        at = lay["rec"]
-        out[at : at + H] = dot_tn(hc[b, 0 : total - n, 0:H], dp[0, n:total]).astype(BF16)
-        out[at + H : at + 2 * H] = dot_tn(hc[b, n:total, H : 2 * H], dp[1, 0 : total - n]).astype(BF16)
-        out[lay["small"] : lay["small"] + 16] = small[...].astype(BF16)
-        active.append(reduces[2 * b + sec])
-        point()
-
-    def stream_grad(r, size):
-        return dot_nt(dp[0, pl.ds(r, size)], wiu[:, 0 : 4 * H]) + dot_nt(
-            dp[1, pl.ds(r, size)], wiu[:, 4 * H : 8 * H]
-        )
+            base = d * lay["half"]
+            out[pl.ds(pl.multiple_of(base + lay["in"], PART), C)] = g[0:C].astype(BF16)
+            small[0:1] = g[C : C + 1]
+            out[pl.ds(pl.multiple_of(base + lay["small"], PART), 16)] = small[...].astype(BF16)
+            h_prev = hc[b, pl.ds(pl.multiple_of(d * n, n), total - n), pl.ds(pl.multiple_of(d * H, H), H)]
+            g = dot_tn(h_prev, dp[d, pl.ds(pl.multiple_of((1 - d) * n, n), total - n)])
+            out[pl.ds(pl.multiple_of(base + lay["rec"], PART), H)] = g.astype(BF16)
+            if d is core:
+                point(0.6)
+            else:
+                reduce.advance(clock[0] + 0.6)
+                active.append(reduce)
+
+    def stream_grad(total):
+        return dot_nt(dp[0, 0:total], wiu[:, 0 : 4 * H]) + dot_nt(dp[1, 0:total], wiu[:, 4 * H : 8 * H])
 
     small[...] = jnp.zeros_like(small)
     for b in reversed(range(blocks)):
@@ -663,22 +705,18 @@
         mx[rows:rows_e] = jnp.zeros((rows_e - rows, LANES), F32)
         for j in range(R):
             dmj[pl.ds(j * kp, kp)] = mx[pl.ds(j, kp, stride=R), :].astype(BF16)
-        run_backward(b, 1, u_e, hc_e, sv_e, kp, R, 2, 2)
-
-        def grad_inter(r):
-            xj[pl.ds(r, rows_e // 4)] = stream_grad(r, rows_e // 4)
-
-        chunks(rows_e, rows_e // 4, grad_inter)
+        run_backward(b, 1, u_e, hc_e, sv_e, kp, R, R, 1)
+
+        xj[...] = stream_grad(rows_e)
         for j in range(R):
             dz[pl.ds(j, kp, stride=R), :] += xj[pl.ds(j * kp, kp)]
+        point(1.5)
 
         norm_backward(b, 0)
-        run_backward(b, 0, u_a, hc_a, sv_a, R, K, 5, 4)
-
-        def grad_intra(r):
-            dz[pl.ds(r, rows // 4)] += stream_grad(r, rows // 4)
-
-        chunks(rows, rows // 4, grad_intra)
+        run_backward(b, 0, u_a, hc_a, sv_a, R, K, 10, 5)
+
+        dz[0:rows] += stream_grad(rows)
+        point(1.5)
 
     def finish(r):
         dz[pl.ds(r, cr)] = dz[pl.ds(r, cr)] * valid[pl.ds(r, cr)]
@@ -687,7 +725,9 @@
     for j in range(R):
         spans_out[j] = dz[pl.ds(j, K, stride=R), :].T[0:C]
     while not all(reduce.over() for reduce in active):
-        point()
+        nearest = min((reduce for reduce in active if not reduce.over()), key=lambda reduce: reduce.due)
+        clock[0] = max(clock[0], nearest.due)
+        nearest.advance(clock[0])
     wave_swap.wait()
     for i in range(wr):
         at = pl.multiple_of(speaker * (wr * LANES) + i * LANES, LANES)
@@ -721,15 +761,17 @@
     speaker = lax.axis_index("spk")
     spans_out[...] = spans_in[...]
     for d in range(2):
-        in_out[d] = sums[lay["in"] + d * C : lay["in"] + (d + 1) * C].astype(F32)
-        rec_out[d] = sums[lay["rec"] + d * H : lay["rec"] + (d + 1) * H].astype(F32)
+        base = d * lay["half"]
+        in_out[d] = sums[base + lay["in"] : base + lay["in"] + C].astype(F32)
+        rec_out[d] = sums[base + lay["rec"] : base + lay["rec"] + H].astype(F32)
+        small = sums[base + lay["small"] : base + lay["small"] + 16].astype(F32)
+        bias_out[d : d + 1] = small[0:1]
+        if d == 0:
+            for m, out in enumerate((proj_bias_out, gain_out, shift_out)):
+                out[b, pl.ds(sec, 1)] = small[1:2, m * LANES : m * LANES + C]
     at = lay["proj"]
     proj_out[0 : C // 2] = sums[at : at + C // 2, 0 : 2 * H].astype(F32)
     proj_out[C // 2 : C] = sums[at : at + C // 2, 2 * H : 4 * H].astype(F32)
-    small = sums[lay["small"] : lay["small"] + 16].astype(F32)
-    bias_out[...] = small[0:2]
-    for m, out in enumerate((proj_bias_out, gain_out, shift_out)):
-        out[b, pl.ds(sec, 1)] = small[2:3, m * LANES : m * LANES + C]
 
     @pl.when(n == 0)
     def _():
@@ -752,10 +794,12 @@
 
 def sum_rows(C, H):
     lay, at = {}, 0
-    for name, rows in (("in", 2 * C), ("rec", 2 * H), ("proj", C // 2), ("small", 16), ("head", 32)):
+    for name, rows in (("in", C), ("rec", H), ("small", 16), ("proj", C // 2)):
         lay[name] = at
         at += rows
-    lay["total"] = -(-at // (32 * PART)) * 32 * PART
+    lay["half"] = -(-at // (16 * PART)) * 16 * PART
+    lay["head"] = lay["half"] + lay["proj"]
+    lay["total"] = 2 * lay["half"]
     return lay
 
 
@@ -790,7 +834,7 @@
 
     sizes = (R, K, C, H, clips, blocks, kp, num_dp)
     lay = sum_rows(C, H)
-    num_hops = num_dp.bit_length()
+    outer = max(num_dp.bit_length() - 5, 0)
     smem = pl.BlockSpec(memory_space=pltpu.SMEM)
     vmem = pl.BlockSpec(memory_space=pltpu.VMEM)
     shape = jax.ShapeDtypeStruct
@@ -818,11 +862,10 @@
             pltpu.VMEM((blocks, rows_e, 2 * H), BF16),
             pltpu.VMEM((blocks, 2, rows, 6 * H), BF16),
             pltpu.VMEM((blocks, 2, rows_e, 6 * H), BF16),
-            pltpu.VMEM((2, rows_e, 4 * H), F32),
+            pltpu.VMEM((2, frames, 2 * LANES), F32),
             pltpu.VMEM((rows_e, 2 * H), F32),
             pltpu.VMEM((2, rows_e, 4 * H), BF16),
-            pltpu.VMEM((LANES, 8 * H), BF16),
-            pltpu.VMEM((2, H, 4 * H), BF16),
+            pltpu.VMEM((2, 2 * H, 4 * H), BF16),
             pltpu.VMEM((LANES, 8 * H), BF16),
             pltpu.VMEM((2, 4 * H, H), BF16),
             pltpu.VMEM((blocks, 2, LANES, 2 * H), BF16),
@@ -840,9 +883,9 @@
             pltpu.VMEM((mask_row, LANES), F32),
             pltpu.SemaphoreType.DMA((4,)),
             pltpu.VMEM((2 * blocks, lay["total"], 4 * H), BF16),
-            pltpu.VMEM((2 * blocks, lay["total"] + PART * max(num_hops - 5, 0), 4 * H), BF16),
+            pltpu.VMEM((2 * blocks, lay["total"] + PART * outer, 4 * H), BF16),
             pltpu.VMEM((16, 4 * H), F32),
-            pltpu.SemaphoreType.DMA((2 * blocks, 2 * num_hops, 2)),
+            pltpu.SemaphoreType.DMA((2 * blocks, 6 + outer, 2)),
         ],
         compiler_params=pltpu.CompilerParams(
             vmem_limit_bytes=62 * 1024 * 1024, collective_id=0, has_side_effects=True
@@ -910,7 +953,7 @@
             whole(1, C),
             whole(2 * half, C),
         ),
-        compiler_params=pltpu.CompilerParams(vmem_limit_bytes=32 * 1024 * 1024),
+        compiler_params=pltpu.CompilerParams(vmem_limit_bytes=60 * 1024 * 1024),
         name="unpack",
     )(outs[2], outs[0], outs[1])
     return (

time: 184 us -> 125 us (0.68)
  Pallas kernels: 179 us -> 124 us
  local copies, waits for them, and re-layouts: 3.43 us -> 0 us
    pallas_call x1, Pallas kernels: 177 us -> 120 us  [shards(): pl.pallas_call(functools.partial(local_kernel, sizes), out_shape=(shape((...]
    unnamed x6 -> x0, local copies, waits for them, and re-layouts: 3.43 us -> none
    pallas_call x1, Pallas kernels: 2.48 us -> 4.37 us  [shards(): pl.pallas_call(functools.partial(unpack_kernel, (C, H)), grid=(2 * blocks...]
where the time goes in v3:
time: 125 us
  Pallas kernels  124 us (99%)
    pallas_call x1, Pallas kernels, shards(): pl.pallas_call(functools.partial(local_kernel, sizes), out_shape=(shape((...  120 us
    pallas_call x1, Pallas kernels, shards(): pl.pallas_call(functools.partial(unpack_kernel, (C, H)), grid=(2 * blocks...  4.37 us

profile of v3, /device:TPU:0, one launch (start us, length us, event | category | flops | bytes accessed | tf_op | source)
XLA Modules:
  0.0 125.3 jit_solution(84274871227717964)
XLA Ops:
  0.7 120.0 %dual_path.1 = (f32[1,12800]{1,0:T(1,128)}, f32[16,64,100]{2,1,0:T(8,128)}, bf16[4,512,512]{2,1,0:T(8,128)(2,1)}) custom-call(s32[1,2,3]{2,1,0:T(2,128)} %lengths_ref.1, s32[1,2,3]{2,1,0:T(2,128)} %pads_ref.1, bf16[16,64,100]{2,1,0:T(8,128)(2,1)} %bitcast.7, bf16[64,800]{1,0:T(8,128)(2,1)} %bitcast.9, bf16[2,2,2,64,512]{4,3,2,1,0:T(8,128)(2,1)} %w_in_ref.1, ...), custom_call_target="tpu_custom_call" | custom-call | tf_op jit(solution)/shard_map/dual_path/pallas_call | solution.py:841
  120.7 4.4 %unpack.1 = (f32[1,12800]{1,0:T(1,128)}, f32[16,64,100]{2,1,0:T(8,128)}, f32[2,2,2,64,512]{4,3,2,1,0:T(8,128)}, f32[2,2,2,128,512]{4,3,2,1,0:T(8,128)}, f32[2,2,...) custom-call(bf16[4,512,512]{2,1,0:T(8,128)(2,1)} %get-tuple-element., ...), custom_call_target="tpu_custom_call" | custom-call | tf_op jit(solution)/shard_map/unpack/pallas_call | solution.py:920
